TPU v7x, 128 devices: a whole 4x4x4 slice. The times are simulated.
128 devices in a mesh: dp: 32 (over x, y, core), tensor: 4 (over z).
Axes of the slice: x: 4, y: 4, z: 4, core: 2. Of those that a mesh axis runs over, the one named last changes fastest.
Arguments:
- flat_weight: bfloat16 [37120, 8192], P(('dp', 'tensor')), may hold values from -0.0625 to 0.0625
- offsets: int32 [5], replicated, may hold values from 0 to 36864, as said below
- group_owner: int32 [8], replicated, may hold values from 0 to 3, as said below
- hidden: bfloat16 [256, 8192], P(None, 'dp'), may hold values from -6 to 6
- decay_rate: float32 [256], replicated, may hold values from 0.003 to 0.12
- dt_bias: float32 [256], replicated, may hold values from -1.5 to 1
- skip_gain: float32 [256], replicated, may hold values from 0.3 to 1.5
- norm_gain: float32 [16384], replicated, may hold values from 0.25 to 1.75
Outputs:
- w_rollout: bfloat16 [8192, 37120], P('dp', 'tensor')
- mixed: bfloat16 [256, 16384], P(None, ('dp', 'tensor'))
Inputs may be any that keep to these rules, and one draw needn't show every extreme that they name: `offsets`: the five segments z, x, B, C, dt, of lengths 16384, 16384, 2048, 2048, 256, lie end to end starting at row 0, z, x, B, C in some order and dt last. `group_owner`: each owner holds exactly 2 groups.
All inputs are finite; a program needn't handle non-finite values.
Results may differ from a plain program's by a relative error of at most 0.002.
Values may be sent and summed in bfloat16 or wider, within the bound.
A program may use at most 128 MiB of HBM per device.

v0:
```python
import jax
import jax.numpy as jnp
from jax import lax
from jax.sharding import PartitionSpec as P

H = 256
P_SIZE = 64
N = 256
G = 8
L = 128


def owner_rows(offsets, group_owner, owner, locals_n, groups_n, group_heads):
    groups = jnp.nonzero(group_owner == owner, size=groups_n)[0].astype(jnp.int32)
    local = jnp.arange(locals_n, dtype=jnp.int32)
    heads = groups[local // group_heads] * group_heads + local % group_heads
    cols = jnp.arange(P_SIZE, dtype=jnp.int32)
    z_rows = offsets[0] + heads[:, None] * P_SIZE + cols[None, :]
    x_rows = offsets[1] + heads[:, None] * P_SIZE + cols[None, :]
    zx_rows = jnp.concatenate([z_rows, x_rows], axis=1).reshape(-1)
    states = jnp.arange(N, dtype=jnp.int32)
    b_rows = (offsets[2] + groups[:, None] * N + states[None, :]).reshape(-1)
    c_rows = (offsets[3] + groups[:, None] * N + states[None, :]).reshape(-1)
    dt_rows = offsets[4] + heads
    return (jnp.concatenate([zx_rows, b_rows, c_rows, dt_rows]).astype(jnp.int32), groups)


def mix_heads(xh, bmat, cmat, dt_raw, rate, bias, skip):
    step = jax.nn.softplus(dt_raw + bias)
    cumul = jnp.cumsum(-rate * step, axis=1)
    diff = cumul[:, :, None, :] - cumul[:, None, :, :]
    length = xh.shape[1]
    lower = jnp.arange(length)[:, None] >= jnp.arange(length)[None, :]
    lower = lower[None, :, :, None]
    decay = jnp.where(lower, jnp.exp(jnp.where(lower, diff, 0.0)), 0.0)
    scores = jnp.einsum("sthn,suhn->stuh", cmat, bmat, precision=lax.Precision.HIGHEST)
    weights = scores * decay * step[:, None, :, :]
    out = jnp.einsum("stuh,suhp->sthp", weights, xh, precision=lax.Precision.HIGHEST)
    return out + skip[None, None, :, None] * xh


def shards(flat_weight, offsets, group_owner, hidden, decay_rate, dt_bias, skip_gain, norm_gain):
    n_data = lax.axis_size("dp")
    n_owner = lax.axis_size("tensor")
    rank_data = lax.axis_index("dp")
    rank_owner = lax.axis_index("tensor")
    group_heads = H // G
    locals_n = H // n_owner
    groups_n = G // n_owner
    dev_heads = locals_n // n_data
    rows_dev = flat_weight.shape[0]
    feat_cols = flat_weight.shape[1] // n_data
    shard = flat_weight.reshape(1, 1, rows_dev, flat_weight.shape[1])
    grouped = lax.all_gather(shard, "tensor", axis=1, tiled=True)
    sliced = lax.all_to_all(grouped, "dp", split_axis=3, concat_axis=0, tiled=True)
    full_rows = sliced.reshape(n_data * n_owner * rows_dev, feat_cols)
    rows, groups = owner_rows(offsets, group_owner, rank_owner, locals_n, groups_n, group_heads)
    w_local = jnp.take(full_rows, rows, axis=0).T
    zx_width = locals_n * 2 * P_SIZE
    tokens_n = hidden.shape[0]
    seqs_n = tokens_n // L
    first_head = rank_data * dev_heads
    proj = jnp.dot(hidden, w_local, preferred_element_type=jnp.float32)
    summed = lax.psum(proj, "dp")
    zx_mine = lax.dynamic_slice_in_dim(summed, first_head * 2 * P_SIZE, dev_heads * 2 * P_SIZE, 1)
    rest = summed[:, zx_width:]
    local_group = first_head // group_heads
    zx = zx_mine.reshape(seqs_n, L, dev_heads, 2, P_SIZE)
    gate = zx[:, :, :, 0, :]
    xh = zx[:, :, :, 1, :]
    bvec = lax.dynamic_slice_in_dim(rest, local_group * N, N, 1)
    cvec = lax.dynamic_slice_in_dim(rest, groups_n * N + local_group * N, N, 1)
    dt_raw = lax.dynamic_slice_in_dim(rest, 2 * groups_n * N + first_head, dev_heads, 1)
    bmat = jnp.broadcast_to(bvec.reshape(seqs_n, L, 1, N), (seqs_n, L, dev_heads, N))
    cmat = jnp.broadcast_to(cvec.reshape(seqs_n, L, 1, N), (seqs_n, L, dev_heads, N))
    heads = (
        groups[local_group] * group_heads
        + first_head % group_heads
        + jnp.arange(dev_heads, dtype=jnp.int32)
    )
    y = mix_heads(
        xh,
        bmat,
        cmat,
        dt_raw.reshape(seqs_n, L, dev_heads),
        decay_rate[heads],
        dt_bias[heads],
        skip_gain[heads],
    )
    v = y * jax.nn.silu(gate)
    squares = jnp.sum(v * v, axis=(2, 3)).reshape(tokens_n, 1)
    onehot = (jnp.arange(groups_n, dtype=jnp.int32)[None, :] == local_group).astype(jnp.float32)
    totals = lax.psum(squares * onehot, "dp")
    total_mine = lax.dynamic_slice_in_dim(totals, local_group, 1, 1)
    scale = lax.rsqrt(total_mine / (group_heads * P_SIZE) + 1e-05)
    gains = norm_gain.reshape(H, P_SIZE)[heads]
    normed = v.reshape(tokens_n, dev_heads, P_SIZE) * scale[:, :, None] * gains[None]
    return (w_local, normed.reshape(tokens_n, dev_heads * P_SIZE).astype(jnp.bfloat16))


def solution(mesh):
    placed = (P(("dp", "tensor"), None), P(), P(), P(None, "dp"), P(), P(), P(), P())
    return jax.shard_map(
        shards,
        mesh=mesh,
        in_specs=placed,
        out_specs=(P("dp", "tensor"), P(None, ("dp", "tensor"))),
        check_vma=False,
    )
```

profile of v0, /device:TPU:1, one launch (start us, length us, event | category | flops | bytes accessed | tf_op | source)
XLA Modules:
  0.0 956.1 jit_solution(2185793429045233098)
XLA Ops:
  7.2 0.7 all-gather.4.cloned.1.call-update
  7.9 182.0 %all-gather.4.cloned.1.call-done = bf16[4,290,8192]{2,1,0:T(8,128)(2,1)} async-done(((bf16[1,290,8192]{2,1,0:T(8,128)(2,1)}), bf16[4,290,8192]{2,1,0:T(8,128)(2,1)}) %all-gather.4.cloned.1.call-update) | async-done | bytes 19005456 | tf_op jit(solution)/shard_map/all_gather | solution.py:54
  189.9 37.0 %copy.24 = bf16[1,4,290,8192]{2,1,0,3:T(4,128)(2,1)} copy(bf16[1,4,290,8192]{3,2,1,0:T(8,128)(2,1)} %bitcast.109) | data formatting | bytes 38010880 | tf_op jit(solution)/shard_map/all_gather | solution.py:54
  226.9 7.7 all-to-all-start
  234.7 0.2 reduce-window.12
  234.9 0.6 scatter_custom_fusion
  235.5 0.2 reduce-window.13
  235.6 0.7 fusion.24
  236.4 0.7 fusion.30
  237.0 1.3 multiply_add_fusion.1
  238.4 0.6 multiply_add_fusion
  239.1 0.7 fusion.29
  239.8 2.0 fusion.34
  241.8 2.7 multiply_add_fusion.2
  244.4 0.1 iota_add_fusion
  244.6 0.1 pad_add_fusion
  244.7 0.1 fusion.9
  244.8 2.0 broadcast_add_fusion
  246.8 0.1 fusion.33
  246.9 346.9 %all-to-all-done = bf16[1,4,290,8192]{2,1,0,3:T(4,128)(2,1)} async-done(((bf16[1,4,290,8192]{2,1,0,3:T(4,128)(2,1)}), bf16[1,4,290,8192]{2,1,0,3:T(4,128)(2,1)}, u32[]{:S(2)}, u32[]{:S(2)}) %all-to-all-start) | async-done | bytes 19005472 | tf_op jit(solution)/shard_map/all_to_all | solution.py:55
  593.8 29.4 %copy.38 = bf16[1,4,290,32,256]{4,3,2,1,0:T(8,128)(2,1)} copy(bf16[1,4,290,32,256]{2,1,4,3,0:T(4,128)(2,1)} %bitcast.15) | data formatting | bytes 38010880 | tf_op jit(solution)/shard_map/all_to_all | solution.py:55
  623.1 18.4 %copy.26 = bf16[32,1,4,290,256]{4,3,2,0,1:T(8,128)(2,1)} copy(bf16[32,1,4,290,256]{4,0,3,2,1:T(8,128)(2,1)} %bitcast.108) | data formatting | bytes 38010880 | tf_op jit(solution)/shard_map/all_to_all | solution.py:55
  641.5 25.3 %reshape.417 = bf16[37120,256]{1,0:T(8,128)(2,1)} reshape(bf16[32,1,4,290,256]{4,3,2,0,1:T(8,128)(2,1)} %copy.26) | data formatting | bytes 38010880 | tf_op jit(solution)/shard_map/reshape | solution.py:56
  666.8 31.1 %gather_fusion = bf16[9280,256]{1,0:T(8,128)(2,1)} fusion(bf16[37120,256]{1,0:T(8,128)(2,1)} %reshape.417, s32[10240]{0:T(1024)S(1)} %pad_clamp_fusion), kind=kCustom, calls=%fused_computation | custom fusion | bytes 9539840 | tf_op jit(solution)/shard_map/jit(_take)/gather | solution.py:58
  697.9 8.9 convolution_bitcast_fusion
  707.5 0.6 gather_fusion.3
  708.2 0.6 gather_fusion.1
  708.8 0.6 gather_fusion.2
  709.5 0.1 reshape.421
  709.6 0.6 gather_fusion.4
  710.1 0.1 mul.163
  710.2 8.0 fusion
  718.2 162.7 %all-reduce.2.cloned.1.call-done = f32[256,9280]{0,1:T(8,128)} async-done(((f32[256,9280]{0,1:T(8,128)}), f32[256,9280]{0,1:T(8,128)}) %all-reduce.2.cloned.1.call-update) | async-done | bytes 9502736 | tf_op jit(solution)/shard_map/psum | solution.py:64
  880.9 1.0 constant_dynamic-slice_fusion.3
  881.9 0.1 reshape.418
  882.1 1.3 slice.46
  883.5 0.1 copy.29
  883.6 0.1 copy.28
  883.7 0.1 broadcast_multiply_fusion
  883.8 0.1 copy.30
  884.0 0.2 reduce_window_sum.25
  884.2 0.1 copy.31
  884.2 0.6 fusion.2
  884.8 0.4 multiply_reduce_fusion
  885.2 0.1 copy.35
  885.4 63.1 %psum.15 = f32[256,2]{0,1:T(2,128)S(1)} all-reduce(f32[256,2]{0,1:T(2,128)S(1)} %broadcast_multiply_fusion.1), channel_id=1, replica_groups=mesh['dp'=32,'tensor'=4] {'dp'}, use_global_device_ids=true, to_apply=%region_7.8 | all-reduce | flops 512 | bytes 4096 | tf_op jit(solution)/shard_map/psum | solution.py:93
  948.5 0.1 fusion.8
  948.6 0.7 copy.36
  (38 shorter events, 0.6 us)
Async XLA Ops:
  7.2 690.8 %copy-start = (bf16[256,256]{1,0:T(8,128)(2,1)S(1)}, bf16[256,256]{1,0:T(8,128)(2,1)}, u32[]{:S(2)}) copy-start(bf16[256,256]{1,0:T(8,128)(2,1)} %param.11) | copy-start | bytes 393220
  7.2 182.7 %all-gather.4.cloned.1.call-start = ((), (), s32[]{:S(2)}) async-start(), calls=%async_computation.2 | async-start | bytes 24248320 | tf_op jit(solution)/shard_map/all_gather | solution.py:54
  226.9 7.8 copy-start.6
  226.9 9.5 copy-start.5
  226.9 366.9 %all-to-all-start = ((bf16[1,4,290,8192]{2,1,0,3:T(4,128)(2,1)}), bf16[1,4,290,8192]{2,1,0,3:T(4,128)(2,1)}, u32[]{:S(2)}, u32[]{:S(2)}) async-start(bf16[1,4,290,8192]{2,1,0,3:T(4,128)(2,1)} %copy.24), calls=%async_computation | async-start | bytes 50331648 | tf_op jit(solution)/shard_map/all_to_all | solution.py:55
  234.6 646.4 %all-reduce.2.cloned.1.call-start = ((), (), s32[]{:S(2)}) async-start(), calls=%async_computation.1 | async-start | bytes 19005440 | tf_op jit(solution)/shard_map/psum | solution.py:64
  706.8 0.7 copy-start.1
  706.8 1.4 copy-start.2
  706.8 2.0 copy-start.3
  706.8 2.7 copy-start.4
Sparse Core Ops, SparseCore 0:
  9.7 180.1 all-gather.3
  707.0 173.9 all-reduce.1
where the time goes:
time: 962 us; the launch traced here: 956 us
  waiting for transfers between devices  692 us (72%)
  local copies, waits for them, and re-layouts  149 us (15%)
  blocking collectives  63.1 us (7%)
  other arithmetic  19.3 us (2%)
  between operations  14.9 us (2%)
  matrix products  9.85 us (1%)
    all_to_all x1, waiting for transfers between devices, shards(): lax.all_to_all(grouped, 'dp', split_axis=3, concat_axis=0, tiled=True)  347 us
    all_gather x1, waiting for transfers between devices, shards(): grouped = lax.all_gather(shard, 'tensor', axis=1, tiled=True)  182 us
    psum x1, waiting for transfers between devices, shards(): summed = lax.psum(proj, 'dp')  163 us
    psum x1, blocking collectives, shards(): totals = lax.psum(squares * onehot, 'dp')  63.1 us
    all_to_all x2, local copies, waits for them, and re-layouts, shards(): lax.all_to_all(grouped, 'dp', split_axis=3, concat_axis=0, tiled=True)  47.8 us
    all_gather x1, local copies, waits for them, and re-layouts, shards(): grouped = lax.all_gather(shard, 'tensor', axis=1, tiled=True)  37 us
    gather x1, local copies, waits for them, and re-layouts, shards(): w_local = jnp.take(full_rows, rows, axis=0).T  31.1 us
    reshape x1, local copies, waits for them, and re-layouts, shards(): full_rows = sliced.reshape(n_data * n_owner * rows_dev, feat_cols)  25.3 us
  transfers between devices with their start and end apart: 3, of which 3 were waited for; matrix products, arithmetic and copies ran while one was open for 2% of the time, Pallas kernels for 0%

commit v1 on v0

--- a/solution.py
+++ b/solution.py
@@ -1,6 +1,11 @@
+import functools
+
 import jax
 import jax.numpy as jnp
+import numpy as np
 from jax import lax
+from jax.experimental import pallas as pl
+from jax.experimental.pallas import tpu as pltpu
 from jax.sharding import PartitionSpec as P
 
 H = 256
@@ -8,21 +13,327 @@
 N = 256
 G = 8
 L = 128
-
-
-def owner_rows(offsets, group_owner, owner, locals_n, groups_n, group_heads):
-    groups = jnp.nonzero(group_owner == owner, size=groups_n)[0].astype(jnp.int32)
-    local = jnp.arange(locals_n, dtype=jnp.int32)
-    heads = groups[local // group_heads] * group_heads + local % group_heads
-    cols = jnp.arange(P_SIZE, dtype=jnp.int32)
-    z_rows = offsets[0] + heads[:, None] * P_SIZE + cols[None, :]
-    x_rows = offsets[1] + heads[:, None] * P_SIZE + cols[None, :]
-    zx_rows = jnp.concatenate([z_rows, x_rows], axis=1).reshape(-1)
-    states = jnp.arange(N, dtype=jnp.int32)
-    b_rows = (offsets[2] + groups[:, None] * N + states[None, :]).reshape(-1)
-    c_rows = (offsets[3] + groups[:, None] * N + states[None, :]).reshape(-1)
-    dt_rows = offsets[4] + heads
-    return (jnp.concatenate([zx_rows, b_rows, c_rows, dt_rows]).astype(jnp.int32), groups)
+ROWS = 290
+D = 8192
+F = 256
+NDP = 32
+NT = 4
+TILE = 16
+CHUNK = 19
+BLOCKS = 18
+BT = 128
+PARTS = (4, 5, 5, 5)
+STARTS = (0, 4, 9, 14)
+MESH = pl.DeviceIdType.MESH
+BF16 = jnp.bfloat16
+F32 = jnp.float32
+
+
+def first_tile(chunk):
+    return ROWS * chunk // TILE
+
+
+def make_tables():
+    n = len(PARTS)
+    lo = np.full((n, NT, BLOCKS), 10**6)
+    hi = np.full((n, NT, BLOCKS), -1)
+    where = {}
+    for k in range(NDP * NT):
+        for l in range(CHUNK):
+            p = max(i for i in range(n) if STARTS[i] <= l)
+            b, tau = divmod(first_tile(k) + l, BT)
+            if b >= BLOCKS:
+                continue
+            i = (k // NT) * PARTS[p] + l - STARTS[p]
+            where.setdefault((b, tau), []).append((k % NT, p, i))
+            lo[p, k % NT, b] = min(lo[p, k % NT, b], i)
+            hi[p, k % NT, b] = max(hi[p, k % NT, b], i)
+    caps = [int((hi[p] - lo[p] + 1).max()) for p in range(n)]
+    start = np.zeros((n, NT, BLOCKS), np.int32)
+    for p in range(n):
+        start[p] = np.clip(lo[p], 0, NDP * PARTS[p] - caps[p])
+    offs = np.concatenate([[0], np.cumsum(caps)])
+    slot = int(offs[-1])
+    place = np.full((BLOCKS, BT, 2), -1, np.int32)
+    for (b, tau), found in where.items():
+        for e, (t, p, i) in enumerate(found):
+            place[b, tau, e] = t * 6 * slot + offs[p] + i - start[p, t, b]
+    return caps, [int(o) for o in offs], slot, start, place
+
+
+CAPS, OFFS, SLOT, START, PLACE = make_tables()
+NP = len(PARTS)
+
+
+def dp_order():
+    steps = [(a, b, c) for a in range(4) for b in range(4) for c in range(2) if (a, b, c) != (0, 0, 0)]
+    steps.sort(key=lambda s: -(min(s[0], 4 - s[0]) + min(s[1], 4 - s[1])))
+    out = []
+    for a, b, c in steps:
+        for q in ((a, b, c), (b, a, c), (-a % 4, -b % 4, c), (-b % 4, -a % 4, c)):
+            if q not in out:
+                out.append(q)
+    return out[::-1]
+
+
+ORDER = dp_order()
+
+
+def dp_partner(d, step):
+    x, y, c = d // 8, (d // 2) % 4, d % 2
+    return ((x + step[0]) % 4) * 8 + ((y + step[1]) % 4) * 2 + (c + step[2]) % 2
+
+
+def owner_groups(owner_ref, owner):
+    first, last = jnp.int32(G), jnp.int32(-1)
+    for g in range(G):
+        mine = owner_ref[g] == owner
+        first = jnp.where(mine, jnp.minimum(first, g), first)
+        last = jnp.where(mine, g, last)
+    return jnp.clip(first, 0, G - 1), jnp.clip(last, 0, G - 1)
+
+
+def prep_kernel(off_ref, own_ref, start_ref, windows_ref):
+    t = lax.axis_index("tensor")
+    seg = [off_ref[i] // 2048 for i in range(4)]
+    for shift in range(NT):
+        g = owner_groups(own_ref, (t + shift) % NT)
+        for p in range(NP):
+            for s in range(4):
+                windows_ref[p * 18 + shift * 4 + s] = start_ref[(p * NT + t) * BLOCKS + seg[s // 2] + g[s % 2]]
+        for i in range(2):
+            windows_ref[NP * 18 + shift * 2 + i] = 2 * g[i]
+    for p in range(NP):
+        for i in range(2):
+            windows_ref[p * 18 + 16 + i] = start_ref[(p * NT + t) * BLOCKS + seg[2 + i]]
+
+
+def prep(offsets, group_owner):
+    smem = pl.BlockSpec(memory_space=pltpu.SMEM)
+    return pl.pallas_call(
+        prep_kernel,
+        out_shape=jax.ShapeDtypeStruct((NP * 18 + 8,), jnp.int32),
+        in_specs=[smem] * 3,
+        out_specs=smem,
+        name="prep",
+    )(offsets, group_owner, jnp.asarray(START.reshape(-1)))
+
+
+def exchange_kernel(windows_ref, flat_ref, out_ref, dt_ref, *scratch):
+    shifted = scratch[:NP]
+    recv = scratch[NP : 2 * NP]
+    send = scratch[2 * NP : 3 * NP]
+    both = scratch[3 * NP : 4 * NP]
+    dtbuf, dtsend, dp_send, dp_recv, z_send, z_recv, self_sem = scratch[4 * NP :]
+    d = lax.axis_index("dp")
+    t = lax.axis_index("tensor")
+
+    barrier = pltpu.get_barrier_semaphore()
+
+    @pl.loop(1, NDP)
+    def _(i):
+        pl.semaphore_signal(barrier, inc=1, device_id=((d + i) % NDP, t), device_id_type=MESH)
+
+    @pl.loop(1, NT)
+    def _(i):
+        pl.semaphore_signal(barrier, inc=1, device_id=(d, (t + i) % NT), device_id_type=MESH)
+
+    pl.semaphore_wait(barrier, NDP - 1 + NT - 1)
+
+    phase = (ROWS * (d * NT + t)) % TILE
+    for p in range(NP):
+        a, rows = STARTS[p] * TILE, PARTS[p] * TILE
+        w0, w1 = max(a - TILE, 0), min(a + rows, ROWS)
+        to = lax.broadcasted_iota(jnp.int32, (rows, w1 - w0), 0) + (a - phase)
+        frm = lax.broadcasted_iota(jnp.int32, (rows, w1 - w0), 1) + w0
+        pick = jnp.where(to == frm, 1.0, 0.0).astype(BF16)
+
+        @pl.loop(0, D // 1024)
+        def _(i):
+            cols = pl.ds(pl.multiple_of(i * 1024, 1024), 1024)
+            moved = jnp.dot(pick, flat_ref[w0:w1, cols], preferred_element_type=F32)
+            shifted[p][:, :, cols] = moved.astype(BF16).reshape(PARTS[p], TILE, 1024)
+
+        mine = pl.ds(d * PARTS[p], PARTS[p])
+        for step in ORDER:
+            peer = dp_partner(d, step)
+            pltpu.make_async_remote_copy(
+                src_ref=shifted[p].at[:, :, pl.ds(pl.multiple_of(peer * F, F), F)],
+                dst_ref=recv[p].at[mine],
+                send_sem=dp_send.at[p],
+                recv_sem=dp_recv.at[p],
+                device_id=(peer, t),
+                device_id_type=MESH,
+            ).start()
+        pltpu.make_async_copy(
+            shifted[p].at[:, :, pl.ds(pl.multiple_of(d * F, F), F)], recv[p].at[mine], dp_recv.at[p]
+        ).start()
+
+    copies = []
+    for p in range(NP):
+        pltpu.make_async_copy(recv[p], recv[p], dp_recv.at[p]).wait()
+
+        def pack(dst, window):
+            first = windows_ref[window]
+
+            @pl.loop(0, CAPS[p], unroll=2)
+            def _(j):
+                dst[j] = recv[p][first + j]
+
+        for i in range(2):
+            pack(both[p].at[i], p * 18 + 16 + i)
+        for l in range(max(STARTS[p], 3), STARTS[p] + PARTS[p]):
+            dtbuf[l - 3] = recv[p][31 * PARTS[p] + l - STARTS[p]]
+        for shift in (1, 3, 2, 0):
+            for s in range(4):
+                pack(send[p].at[shift, s], p * 18 + shift * 4 + s)
+            target = (d, (t + shift) % NT)
+            span = pl.ds(OFFS[p], CAPS[p])
+            pairs = [
+                (send[p].at[shift], out_ref.at[t, 0:4, span]),
+                (both[p], out_ref.at[t, 4:6, span]),
+            ]
+            for n, (src, dst) in enumerate(pairs):
+                if shift == 0:
+                    cp = pltpu.make_async_copy(src, dst, self_sem.at[2 * p + n])
+                else:
+                    cp = pltpu.make_async_remote_copy(
+                        src_ref=src,
+                        dst_ref=dst,
+                        send_sem=z_send.at[shift - 1, 2 * p + n],
+                        recv_sem=z_recv.at[shift - 1, 2 * p + n],
+                        device_id=target,
+                        device_id_type=MESH,
+                    )
+                cp.start()
+                copies.append(cp)
+    for shift in (1, 3, 2, 0):
+        for i in range(2):
+            for j in range(2):
+                dtsend[shift, 2 * i + j] = dtbuf[windows_ref[NP * 18 + shift * 2 + i] + j]
+        if shift == 0:
+            cp = pltpu.make_async_copy(dtsend.at[0], dt_ref.at[t], self_sem.at[2 * NP])
+        else:
+            cp = pltpu.make_async_remote_copy(
+                src_ref=dtsend.at[shift],
+                dst_ref=dt_ref.at[t],
+                send_sem=z_send.at[shift - 1, 2 * NP],
+                recv_sem=z_recv.at[shift - 1, 2 * NP],
+                device_id=(d, (t + shift) % NT),
+                device_id_type=MESH,
+            )
+        cp.start()
+        copies.append(cp)
+    for cp in copies:
+        cp.wait()
+    for p in range(NP):
+        sent = shifted[p].at[:, :, 0 : (NDP - 1) * F]
+        pltpu.make_async_copy(sent, sent, dp_send.at[p]).wait()
+
+
+def exchange(windows, flat):
+    any_ = pl.BlockSpec(memory_space=pl.ANY)
+    return pl.pallas_call(
+        exchange_kernel,
+        out_shape=(
+            jax.ShapeDtypeStruct((NT, 6, SLOT, TILE, F), BF16),
+            jax.ShapeDtypeStruct((NT, 4, TILE, F), BF16),
+        ),
+        in_specs=[pl.BlockSpec(memory_space=pltpu.SMEM), pl.BlockSpec(memory_space=pltpu.VMEM)],
+        out_specs=(any_, any_),
+        scratch_shapes=[pltpu.VMEM((w, TILE, D), BF16) for w in PARTS]
+        + [pltpu.VMEM((NDP * w, TILE, F), BF16) for w in PARTS]
+        + [pltpu.VMEM((NT, 4, c, TILE, F), BF16) for c in CAPS]
+        + [pltpu.VMEM((2, c, TILE, F), BF16) for c in CAPS]
+        + [
+            pltpu.VMEM((16, TILE, F), BF16),
+            pltpu.VMEM((NT, 4, TILE, F), BF16),
+            pltpu.SemaphoreType.DMA((NP,)),
+            pltpu.SemaphoreType.DMA((NP,)),
+            pltpu.SemaphoreType.DMA((NT - 1, 2 * NP + 1)),
+            pltpu.SemaphoreType.DMA((NT - 1, 2 * NP + 1)),
+            pltpu.SemaphoreType.DMA((2 * NP + 1,)),
+        ],
+        compiler_params=pltpu.CompilerParams(
+            collective_id=1, has_side_effects=True, vmem_limit_bytes=56 << 20
+        ),
+        name="exchange",
+    )(windows, flat)
+
+
+WIDE = 1024
+
+
+def place_kernel(off_ref, own_ref, place_ref, got_ref, dt_ref, out_ref, rows_ref):
+    step = pl.program_id(0)
+    g = owner_groups(own_ref, lax.axis_index("tensor"))
+    eye = jnp.where(
+        lax.broadcasted_iota(jnp.int32, (F, F), 0) == lax.broadcasted_iota(jnp.int32, (F, F), 1), 1.0, 0.0
+    ).astype(BF16)
+
+    def tile(slot, block, tau):
+        at = (block * BT + tau) * 2
+        one, two = place_ref[at], place_ref[at + 1]
+        base = slot * SLOT
+        first = got_ref[one + base]
+        second = got_ref[jnp.maximum(two, 0) + base]
+        return first + jnp.where(two >= 0, second, jnp.zeros_like(second))
+
+    def emit(width):
+        out_ref[:, :width] = lax.dot_general(
+            eye, rows_ref[:width], (((1,), (1,)), ((), ())), preferred_element_type=F32
+        ).astype(BF16)
+
+    @pl.when(step < 8)
+    def _():
+        k = step // 4
+        gk = jnp.where(k == 0, g[0], g[1])
+        for seg in range(2):
+            block = off_ref[seg] // 2048 + gk
+            for j in range(8):
+                u = (step % 4) * 8 + j
+                for q in range(4):
+                    r = j * 128 + seg * 64 + q * TILE
+                    rows_ref[r : r + TILE] = tile(2 * seg + k, block, 4 * u + q)
+        emit(WIDE)
+
+    @pl.when(step == 8)
+    def _():
+        for seg in range(2):
+            block = off_ref[2 + seg] // 2048
+            for k in range(2):
+                for q in range(16):
+                    r = (seg * 2 + k) * 256 + q * TILE
+                    rows_ref[r : r + TILE] = tile(4 + seg, block, g[k] * 16 + q)
+        emit(WIDE)
+
+    @pl.when(step == 9)
+    def _():
+        for j in range(4):
+            rows_ref[j * TILE : (j + 1) * TILE] = dt_ref[3, j]
+        emit(128)
+
+
+def place(offsets, group_owner, got, dt):
+    smem = pl.BlockSpec(memory_space=pltpu.SMEM)
+    table = jnp.asarray(PLACE.reshape(-1))
+    got = got.reshape(NT * 6 * SLOT, TILE, F)
+    return pl.pallas_call(
+        place_kernel,
+        grid=(10,),
+        out_shape=jax.ShapeDtypeStruct((F, 9280), BF16),
+        in_specs=[
+            smem,
+            smem,
+            smem,
+            pl.BlockSpec((NT * 6 * SLOT, TILE, F), lambda i: (0, 0, 0)),
+            pl.BlockSpec((NT, 4, TILE, F), lambda i: (0, 0, 0, 0)),
+        ],
+        out_specs=pl.BlockSpec((F, WIDE), lambda i: (0, i)),
+        scratch_shapes=[pltpu.VMEM((WIDE, F), BF16)],
+        compiler_params=pltpu.CompilerParams(vmem_limit_bytes=48 << 20),
+        name="place",
+    )(offsets, group_owner, table, got, dt)
 
 
 def mix_heads(xh, bmat, cmat, dt_raw, rate, bias, skip):
@@ -48,14 +359,9 @@
     locals_n = H // n_owner
     groups_n = G // n_owner
     dev_heads = locals_n // n_data
-    rows_dev = flat_weight.shape[0]
-    feat_cols = flat_weight.shape[1] // n_data
-    shard = flat_weight.reshape(1, 1, rows_dev, flat_weight.shape[1])
-    grouped = lax.all_gather(shard, "tensor", axis=1, tiled=True)
-    sliced = lax.all_to_all(grouped, "dp", split_axis=3, concat_axis=0, tiled=True)
-    full_rows = sliced.reshape(n_data * n_owner * rows_dev, feat_cols)
-    rows, groups = owner_rows(offsets, group_owner, rank_owner, locals_n, groups_n, group_heads)
-    w_local = jnp.take(full_rows, rows, axis=0).T
+    got, dt_rows = exchange(prep(offsets, group_owner), flat_weight)
+    w_local = place(offsets, group_owner, got, dt_rows)
+    groups = jnp.nonzero(group_owner == rank_owner, size=groups_n)[0].astype(jnp.int32)
     zx_width = locals_n * 2 * P_SIZE
     tokens_n = hidden.shape[0]
     seqs_n = tokens_n // L

time: 962 us -> 339 us (0.35)
  waiting for transfers between devices: 692 us -> 108 us
  local copies, waits for them, and re-layouts: 149 us -> 17.9 us
  Pallas kernels: 0 us -> 122 us
  other arithmetic: 19.3 us -> 2.75 us
    all_to_all x1 -> x0, waiting for transfers between devices: 347 us -> none  [shards(): lax.all_to_all(grouped, 'dp', split_axis=3, concat_axis=0, tiled=True)]
    all_gather x1 -> x0, waiting for transfers between devices: 182 us -> none  [shards(): grouped = lax.all_gather(shard, 'tensor', axis=1, tiled=True)]
    pallas_call x0 -> x3, Pallas kernels: none -> 122 us  [the longest x1 112 us: exchange(): pl.pallas_call(exchange_kernel, out_shape=(jax.ShapeDtypeStruct((NT, 6, S...]
    psum x1, waiting for transfers between devices: 163 us -> 108 us  [shards(): summed = lax.psum(proj, 'dp')]
    all_to_all x2 -> x0, local copies, waits for them, and re-layouts: 47.8 us -> none  [shards(): lax.all_to_all(grouped, 'dp', split_axis=3, concat_axis=0, tiled=True)]
    all_gather x1 -> x0, local copies, waits for them, and re-layouts: 37 us -> none  [shards(): grouped = lax.all_gather(shard, 'tensor', axis=1, tiled=True)]
    gather x1 -> x0, local copies, waits for them, and re-layouts: 31.1 us -> none  [shards(): w_local = jnp.take(full_rows, rows, axis=0).T]
    reshape x1 -> x0, local copies, waits for them, and re-layouts: 25.3 us -> none  [shards(): full_rows = sliced.reshape(n_data * n_owner * rows_dev, feat_cols)]
  transfers between devices with their start and end apart: 3 -> 1, of which waited for: 3 -> 1; matrix products, arithmetic and copies ran while one was open for 2% -> 4% of each run, Pallas kernels for 0% -> 0%
where the time goes in v1:
time: 339 us; the launch traced here: 336 us
  Pallas kernels  122 us (36%)
  waiting for transfers between devices  108 us (32%)
  blocking collectives  63.1 us (19%)
  local copies, waits for them, and re-layouts  17.9 us (5%)
  between operations  15 us (4%)
  matrix products  6.78 us (2%)
    pallas_call x1, Pallas kernels, exchange(): pl.pallas_call(exchange_kernel, out_shape=(jax.ShapeDtypeStruct((NT, 6, S...  112 us
    psum x1, waiting for transfers between devices, shards(): summed = lax.psum(proj, 'dp')  108 us
    psum x1, blocking collectives, shards(): totals = lax.psum(squares * onehot, 'dp')  63.1 us
    unnamed x23, local copies, waits for them, and re-layouts  11.6 us
    pallas_call x1, Pallas kernels, place(): pl.pallas_call(place_kernel, grid=(10,), out_shape=jax.ShapeDtypeStruct((...  9.24 us
  transfers between devices with their start and end apart: 1, of which 1 were waited for; matrix products, arithmetic and copies ran while one was open for 4% of the time, Pallas kernels for 0%

profile of v1, /device:TPU:1, one launch (start us, length us, event | category | flops | bytes accessed | tf_op | source)
XLA Modules:
  0.0 335.6 jit_solution(18357851778349965173)
XLA Ops:
  7.2 0.0 copy-start
  7.2 0.0 copy-start.3
  7.2 0.0 all-reduce.2.cloned.1.call-start
  7.3 1.5 prep.1.windows_ref
  8.8 111.6 %exchange.1 = (bf16[4,6,38,16,256]{4,3,2,1,0:T(8,128)(2,1)}, bf16[4,4,16,256]{3,2,1,0:T(8,128)(2,1)}) custom-call(s32[80]{0:T(128)} %prep.1.windows_ref, bf16[290,8192]{1,0:T(8,128)(2,1)} %flat_ref.1), custom_call_target="tpu_custom_call" | custom-call | tf_op jit(solution)/shard_map/exchange/pallas_call | solution.py:236
  120.4 0.9 copy-done.2
  121.3 9.2 %place.1 = bf16[256,9280]{1,0:T(8,128)(2,1)S(1)} custom-call(s32[5]{0:T(128)S(1)} %copy-done.4, s32[8]{0:T(128)S(1)} %copy-done.5, s32[4608]{0:T(1024)S(1)} %copy-done.3, bf16[912,16,256]{2,1,0:T(8,128)(2,1)} %bitcast.62, bf16[4,4,16,256]{3,2,1,0:T(8,128)(2,1)S(1)} %copy-done.2), custom_call_target="tpu_custom_call" | custom-call | tf_op jit(solution)/shard_map/place/pallas_call | solution.py:321
  130.6 0.0 copy-start.1
  130.6 2.2 copy-done.1
  132.8 5.1 %convolution_bitcast_fusion = f32[256,9280]{0,1:T(8,128)} fusion(bf16[256,9280]{1,0:T(8,128)(2,1)S(1)} %place.1, bf16[256,256]{1,0:T(8,128)(2,1)S(1)} %copy-done), kind=kOutput, calls=%fused_computation.5 | convolution fusion | flops 1216348160 | bytes 14385152 | tf_op jit(solution)/shard_map/dot_general | solution.py:369
  137.9 0.0 all-reduce.2.cloned.1.call-update
  137.9 0.0 copy-start.6
  137.9 0.0 copy-start.7
  137.9 0.0 copy-start.8
  138.0 0.0 copy-start.9
  138.0 7.6 %copy.24 = bf16[256,9280]{0,1:T(8,128)(2,1)} copy(bf16[256,9280]{1,0:T(8,128)(2,1)} %copy-done.1) | data formatting | bytes 9502720
  145.6 0.2 reduce-window.14
  145.8 0.6 scatter_custom_fusion
  146.4 0.2 reduce-window.15
  146.6 0.6 fusion.15
  147.2 0.7 compare_select_fusion.5
  147.9 0.6 dynamic_slice.21
  149.2 0.6 gather_fusion.2
  149.8 0.0 copy-done.7
  149.8 0.6 gather_fusion
  150.5 0.6 gather_fusion.1
  151.1 0.0 copy-done.9
  151.1 0.1 reshape.145
  151.2 0.6 gather_fusion.3
  151.8 0.1 mul.113
  151.9 107.8 %all-reduce.2.cloned.1.call-done = f32[256,9280]{0,1:T(8,128)} async-done(((f32[256,9280]{0,1:T(8,128)}), f32[256,9280]{0,1:T(8,128)}) %all-reduce.2.cloned.1.call-update) | async-done | bytes 9502736 | tf_op jit(solution)/shard_map/psum | solution.py:370
  259.6 1.0 constant_dynamic-slice_fusion.3
  260.6 0.1 reshape.139
  260.8 1.3 slice.21
  262.1 0.1 copy.18
  262.3 0.1 copy.31
  262.4 0.1 copy.32
  262.5 0.1 broadcast_multiply_fusion
  262.6 0.1 copy.19
  262.8 0.2 reduce_window_sum.25
  263.0 0.1 copy.20
  263.1 1.0 fusion.1
  264.1 0.6 multiply_reduce_fusion
  264.7 0.1 copy.23
  264.8 0.1 broadcast_multiply_fusion.1
  264.9 63.1 %psum.15 = f32[256,2]{0,1:T(2,128)S(1)} all-reduce(f32[256,2]{0,1:T(2,128)S(1)} %broadcast_multiply_fusion.1), channel_id=1, replica_groups=mesh['dp'=32,'tensor'=4] {'dp'}, use_global_device_ids=true, to_apply=%region_7.8 | all-reduce | flops 512 | bytes 4096 | tf_op jit(solution)/shard_map/psum | solution.py:399
  328.0 0.1 fusion.7
  328.1 0.7 copy.25
  (20 shorter events, 0.1 us)
Async XLA Ops:
  7.2 125.6 %copy-start = (bf16[256,256]{1,0:T(8,128)(2,1)S(1)}, bf16[256,256]{1,0:T(8,128)(2,1)}, u32[]{:S(2)}) copy-start(bf16[256,256]{1,0:T(8,128)(2,1)} %param.13) | copy-start | bytes 393220
  7.2 113.2 %copy-start.3 = (s32[4608]{0:T(1024)S(1)}, s32[4608]{0:T(1024)}, u32[]{:S(2)}) copy-start(s32[4608]{0:T(1024)} %constant.113.clone.place_ref) | copy-start | bytes 55300
  7.2 113.2 %copy-start.4 = (s32[5]{0:T(128)S(1)}, s32[5]{0:T(128)}, u32[]{:S(2)}) copy-start(s32[5]{0:T(128)} %off_ref.3) | copy-start | bytes 64
  7.2 113.2 %copy-start.5 = (s32[8]{0:T(128)S(1)}, s32[8]{0:T(128)}, u32[]{:S(2)}) copy-start(s32[8]{0:T(128)} %own_ref.3) | copy-start | bytes 100
  7.2 252.4 %all-reduce.2.cloned.1.call-start = ((), (), s32[]{:S(2)}) async-start(), calls=%async_computation | async-start | bytes 19005440 | tf_op jit(solution)/shard_map/psum | solution.py:370
  120.4 0.9 copy-start.2
  130.6 2.2 copy-start.1
  137.9 11.2 %copy-start.6 = (f32[256]{0:T(256)S(1)}, f32[256]{0:T(256)}, u32[]{:S(2)}) copy-start(f32[256]{0:T(256)} %param.16) | copy-start | bytes 3076
  137.9 11.9 %copy-start.7 = (f32[256]{0:T(256)S(1)}, f32[256]{0:T(256)}, u32[]{:S(2)}) copy-start(f32[256]{0:T(256)} %param.14) | copy-start | bytes 3076
  137.9 12.5 %copy-start.8 = (f32[256]{0:T(256)S(1)}, f32[256]{0:T(256)}, u32[]{:S(2)}) copy-start(f32[256]{0:T(256)} %param.15) | copy-start | bytes 3076
  138.0 13.1 %copy-start.9 = (f32[16384]{0:T(1024)S(1)}, f32[16384]{0:T(1024)}, u32[]{:S(2)}) copy-start(f32[16384]{0:T(1024)} %param.17) | copy-start | bytes 196612
Sparse Core Ops, SparseCore 0:
  138.0 121.5 all-reduce.1

commit v2 on v1

v2 whole, which is shorter than its diff:
```python
import functools

import jax
import jax.numpy as jnp
import numpy as np
from jax import lax
from jax.experimental import pallas as pl
from jax.experimental.pallas import tpu as pltpu
from jax.sharding import PartitionSpec as P

H = 256
P_SIZE = 64
N = 256
G = 8
L = 128
ROWS = 290
D = 8192
F = 256
NDP = 32
NT = 4
TILE = 16
CHUNK = 19
BLOCKS = 18
BT = 128
PARTS = (4, 5, 5, 5)
STARTS = (0, 4, 9, 14)
MESH = pl.DeviceIdType.MESH
BF16 = jnp.bfloat16
F32 = jnp.float32


def first_tile(chunk):
    return ROWS * chunk // TILE


def make_tables():
    n = len(PARTS)
    lo = np.full((n, NT, BLOCKS), 10**6)
    hi = np.full((n, NT, BLOCKS), -1)
    where = {}
    for k in range(NDP * NT):
        for l in range(CHUNK):
            p = max(i for i in range(n) if STARTS[i] <= l)
            b, tau = divmod(first_tile(k) + l, BT)
            if b >= BLOCKS:
                continue
            i = (k // NT) * PARTS[p] + l - STARTS[p]
            where.setdefault((b, tau), []).append((k % NT, p, i))
            lo[p, k % NT, b] = min(lo[p, k % NT, b], i)
            hi[p, k % NT, b] = max(hi[p, k % NT, b], i)
    caps = [int((hi[p] - lo[p] + 1).max()) for p in range(n)]
    start = np.zeros((n, NT, BLOCKS), np.int32)
    for p in range(n):
        start[p] = np.clip(lo[p], 0, NDP * PARTS[p] - caps[p])
    offs = np.concatenate([[0], np.cumsum(caps)])
    slot = int(offs[-1])
    place = np.full((BLOCKS, BT, 2), -1, np.int32)
    for (b, tau), found in where.items():
        for e, (t, p, i) in enumerate(found):
            place[b, tau, e] = t * 6 * slot + offs[p] + i - start[p, t, b]
    return caps, [int(o) for o in offs], slot, start, place


PICKS = 3
PT = 6 * PICKS + 1
ZERO2 = 2 * NDP
ZERO3 = NT * PT


def make_product_tables():
    pick = np.full((NT, 16, BLOCKS, PICKS), ZERO2, np.int32)
    merge = np.full((16, BLOCKS, 8, 2), -1, np.int32)
    count = np.zeros((NT, 16, BLOCKS), np.int32)
    seen = np.zeros((16, BLOCKS, 8), np.int32)
    for k in range(NDP * NT):
        for l in range(CHUNK):
            tile = first_tile(k) + l
            b, tau = divmod(tile, BT)
            if b >= BLOCKS:
                continue
            t, e, m = k % NT, tau % 16, tau // 16
            n = count[t, e, b]
            pick[t, e, b, n] = (k // NT) * 2 + l // 16
            merge[e, b, m, seen[e, b, m]] = t * PT + n
            count[t, e, b] += 1
            seen[e, b, m] += 1
    return pick, merge


CAPS, OFFS, SLOT, START, PLACE = make_tables()
PICK, MERGE = make_product_tables()
NP = len(PARTS)
W_DT = NP * 18
W_PICK = W_DT + 8
W_MERGE = W_PICK + 18 * PICKS
W_HEAD = W_MERGE + 72
W_SIZE = W_HEAD + 3


def dp_order():
    steps = [(a, b, c) for a in range(4) for b in range(4) for c in range(2) if (a, b, c) != (0, 0, 0)]
    steps.sort(key=lambda s: -(min(s[0], 4 - s[0]) + min(s[1], 4 - s[1])))
    out = []
    for a, b, c in steps:
        for q in ((a, b, c), (b, a, c), (-a % 4, -b % 4, c), (-b % 4, -a % 4, c)):
            if q not in out:
                out.append(q)
    return out[::-1]


ORDER = dp_order()


def dp_partner(d, step):
    x, y, c = d // 8, (d // 2) % 4, d % 2
    return ((x + step[0]) % 4) * 8 + ((y + step[1]) % 4) * 2 + (c + step[2]) % 2


def owner_groups(owner_ref, owner):
    first, last = jnp.int32(G), jnp.int32(-1)
    for g in range(G):
        mine = owner_ref[g] == owner
        first = jnp.where(mine, jnp.minimum(first, g), first)
        last = jnp.where(mine, g, last)
    return jnp.clip(first, 0, G - 1), jnp.clip(last, 0, G - 1)


def prep_kernel(off_ref, own_ref, start_ref, pick_ref, merge_ref, windows_ref):
    d = lax.axis_index("dp")
    t = lax.axis_index("tensor")
    e = d // 2
    seg = [off_ref[i] // 2048 for i in range(4)]

    def picks(at, b):
        for n in range(PICKS):
            windows_ref[at + n] = pick_ref[((t * 16 + e) * BLOCKS + b) * PICKS + n]

    for shift in range(NT):
        g = owner_groups(own_ref, (t + shift) % NT)
        for s in range(4):
            b = seg[s // 2] + g[s % 2]
            for p in range(NP):
                windows_ref[p * 18 + shift * 4 + s] = start_ref[(p * NT + t) * BLOCKS + b]
            picks(W_PICK + (shift * 4 + s) * PICKS, b)
        for i in range(2):
            windows_ref[W_DT + shift * 2 + i] = 2 * g[i]
    for i in range(2):
        for p in range(NP):
            windows_ref[p * 18 + 16 + i] = start_ref[(p * NT + t) * BLOCKS + seg[2 + i]]
        picks(W_PICK + (16 + i) * PICKS, seg[2 + i])

    def merged(at, b, m, slot):
        for n in range(2):
            v = merge_ref[((e * BLOCKS + b) * 8 + m) * 2 + n]
            windows_ref[at + n] = jnp.where(v < 0, ZERO3, v + PICKS * slot)

    g = owner_groups(own_ref, t)
    for s in range(4):
        for m in range(8):
            merged(W_MERGE + (s * 8 + m) * 2, seg[s // 2] + g[s % 2], m, s)
    for i in range(2):
        for k in range(2):
            merged(W_MERGE + 64 + (i * 2 + k) * 2, seg[2 + i], g[k], 4 + i)
    mine = jnp.where(d < 16, g[0], g[1])
    windows_ref[W_HEAD] = 2 * mine + (d % 16) // 8
    windows_ref[W_HEAD + 1] = 32 * mine + 2 * (d % 16)
    windows_ref[W_HEAD + 2] = 16 * mine + d % 16


def prep(offsets, group_owner):
    smem = pl.BlockSpec(memory_space=pltpu.SMEM)
    return pl.pallas_call(
        prep_kernel,
        out_shape=jax.ShapeDtypeStruct((W_SIZE,), jnp.int32),
        in_specs=[smem] * 5,
        out_specs=smem,
        name="prep",
    )(
        offsets,
        group_owner,
        jnp.asarray(START.reshape(-1)),
        jnp.asarray(PICK.reshape(-1)),
        jnp.asarray(MERGE.reshape(-1)),
    )


def iota(shape, dim):
    return lax.broadcasted_iota(jnp.int32, shape, dim)


def exchange_kernel(
    windows_ref, rate_ref, bias_ref, skip_ref, gain_ref, hidden_ref, flat_ref, out_ref, dt_ref, mixed_ref, *scratch
):
    shifted = scratch[:NP]
    recv = scratch[NP : 2 * NP]
    send = scratch[2 * NP : 3 * NP]
    both = scratch[3 * NP : 4 * NP]
    dtbuf, dtsend, dp_send, dp_recv, z_send, z_recv, self_sem = scratch[4 * NP : 4 * NP + 7]
    hid, prod, precv, zsend, zcom, zrecv, hsend, hrecv, bsend, brecv, qsend, qrecv = scratch[4 * NP + 7 : 4 * NP + 19]
    ag_send, ag_recv, p_send, p_recv, zp_send, zp_recv, own_sem = scratch[4 * NP + 19 :]
    d = lax.axis_index("dp")
    t = lax.axis_index("tensor")
    x, y, c = d // 8, (d // 2) % 4, d % 2
    e, seq = d // 2, d % 2
    chunk = d * NT + t

    barrier = pltpu.get_barrier_semaphore()

    @pl.loop(1, NDP)
    def _(i):
        pl.semaphore_signal(barrier, inc=1, device_id=((d + i) % NDP, t), device_id_type=MESH)

    @pl.loop(1, NT)
    def _(i):
        pl.semaphore_signal(barrier, inc=1, device_id=(d, (t + i) % NT), device_id_type=MESH)

    pl.semaphore_wait(barrier, NDP - 1 + NT - 1)

    def remote(src, dst, ssem, rsem, device):
        cp = pltpu.make_async_remote_copy(
            src_ref=src, dst_ref=dst, send_sem=ssem, recv_sem=rsem, device_id=device, device_id_type=MESH
        )
        cp.start()
        return cp

    def await_bytes(ref, sem):
        pltpu.make_async_copy(ref, ref, sem).wait()

    copies = []

    phase = (ROWS * chunk) % TILE

    def shift_part(p):
        a, rows = STARTS[p] * TILE, PARTS[p] * TILE
        w0, w1 = max(a - TILE, 0), min(a + rows, ROWS)
        pick = jnp.where(iota((rows, w1 - w0), 0) + (a - phase) == iota((rows, w1 - w0), 1) + w0, 1.0, 0.0)
        pick = pick.astype(BF16)

        @pl.loop(0, D // 1024)
        def _(i):
            cols = pl.ds(pl.multiple_of(i * 1024, 1024), 1024)
            moved = jnp.dot(pick, flat_ref[w0:w1, cols], preferred_element_type=F32)
            shifted[p][:, :, cols] = moved.astype(BF16).reshape(PARTS[p], TILE, 1024)

    def send_part(p):
        mine = pl.ds(d * PARTS[p], PARTS[p])
        for step in ORDER:
            peer = dp_partner(d, step)
            remote(
                shifted[p].at[:, :, pl.ds(pl.multiple_of(peer * F, F), F)],
                recv[p].at[mine],
                dp_send.at[p],
                dp_recv.at[p],
                (peer, t),
            )
        pltpu.make_async_copy(
            shifted[p].at[:, :, pl.ds(pl.multiple_of(d * F, F), F)], recv[p].at[mine], dp_recv.at[p]
        ).start()

    def forward_part(p):
        await_bytes(recv[p], dp_recv.at[p])

        def pack(dst, window):
            first = windows_ref[window]

            @pl.loop(0, CAPS[p], unroll=2)
            def _(j):
                dst[j] = recv[p][first + j]

        for i in range(2):
            pack(both[p].at[i], p * 18 + 16 + i)
        for l in range(max(STARTS[p], 3), STARTS[p] + PARTS[p]):
            dtbuf[l - 3] = recv[p][31 * PARTS[p] + l - STARTS[p]]
        for shift in (1, 3, 2, 0):
            for s in range(4):
                pack(send[p].at[shift, s], p * 18 + shift * 4 + s)
            span = pl.ds(OFFS[p], CAPS[p])
            pairs = [(send[p].at[shift], out_ref.at[t, 0:4, span]), (both[p], out_ref.at[t, 4:6, span])]
            for n, (src, dst) in enumerate(pairs):
                if shift == 0:
                    cp = pltpu.make_async_copy(src, dst, self_sem.at[2 * p + n])
                    cp.start()
                else:
                    cp = remote(
                        src,
                        dst,
                        z_send.at[shift - 1, 2 * p + n],
                        z_recv.at[shift - 1, 2 * p + n],
                        (d, (t + shift) % NT),
                    )
                copies.append(cp)

    def forward_dt():
        for shift in (1, 3, 2, 0):
            for i in range(2):
                for j in range(2):
                    dtsend[shift, 2 * i + j] = dtbuf[windows_ref[W_DT + shift * 2 + i] + j]
            if shift == 0:
                cp = pltpu.make_async_copy(dtsend.at[0], dt_ref.at[t], self_sem.at[2 * NP])
                cp.start()
            else:
                cp = remote(
                    dtsend.at[shift],
                    dt_ref.at[t],
                    z_send.at[shift - 1, 2 * NP],
                    z_recv.at[shift - 1, 2 * NP],
                    (d, (t + shift) % NT),
                )
            copies.append(cp)

    def along_x(i):
        return (((x + i) % 4) * 8 + y * 2 + c, t)

    def along_y(i):
        return (x * 8 + ((y + i) % 4) * 2 + c, t)

    def gather_first():
        own = pltpu.make_async_copy(hidden_ref, hid.at[x, y, c], own_sem.at[0])
        own.start()
        for i in (1, 3, 2):
            remote(hidden_ref.at[0:L], hid.at[x, y, c, 0:L], ag_send.at[0], ag_recv.at[0], along_x(i))
            remote(hidden_ref.at[L:], hid.at[x, y, c, L:], ag_send.at[1], ag_recv.at[1], along_y(i))
        own.wait()

    def gather_second():
        await_bytes(hid.at[0:3, 0, 0, 0:L], ag_recv.at[0])
        for i in (1, 3, 2):
            remote(hid.at[:, y, c, 0:L], hid.at[:, y, c, 0:L], ag_send.at[2], ag_recv.at[2], along_y(i))
        await_bytes(hid.at[0:3, 0, 0, L:], ag_recv.at[1])
        for i in (1, 3, 2):
            remote(hid.at[x, :, c, L:], hid.at[x, :, c, L:], ag_send.at[3], ag_recv.at[3], along_x(i))

    def gather_third():
        await_bytes(hid.at[0:3, :, 0, 0:L], ag_recv.at[2])
        await_bytes(hid.at[0:3, :, 0, L:], ag_recv.at[3])
        remote(hid.at[:, :, c], hid.at[:, :, c], ag_send.at[4], ag_recv.at[4], (d + 1 - 2 * c, t))
        await_bytes(hid.at[:, :, 0], ag_recv.at[4])

    def multiply():
        prod[...] = jnp.zeros_like(prod)

        @pl.loop(0, NDP)
        def _(i):
            cols = pl.ds(pl.multiple_of(i * F, F), F)
            rows = jnp.concatenate(
                [shifted[p][:, :, cols].reshape(PARTS[p] * TILE, F) for p in range(NP)], axis=0
            )
            part = lax.dot_general(
                rows, hid[i // 8, (i // 2) % 4, i % 2], (((1,), (1,)), ((), ())), preferred_element_type=F32
            )
            for s in range(2):
                prod[s, 0:CHUNK] += part[:, s * L : (s + 1) * L].reshape(CHUNK, TILE, L)

    def product_tiles(i):
        low = (i // 2 + 16 * NDP * NT * CHUNK - first_tile(chunk)) % 16
        return low, i % 2

    def send_products():
        @pl.loop(1, NDP)
        def _(n):
            i = (d + n) % NDP
            low, s = product_tiles(i)
            for h in range(2):
                remote(prod.at[s, low + 16 * h], precv.at[2 * d + h], p_send.at[0], p_recv.at[0], (i, t))

        low, s = product_tiles(d)
        for h in range(2):
            pltpu.make_async_copy(prod.at[s, low + 16 * h], precv.at[2 * d + h], p_recv.at[0]).start()

    def forward_products():
        await_bytes(precv.at[0 : 2 * NDP], p_recv.at[0])
        for n in range(2 * PICKS):
            zcom[n] = precv[windows_ref[W_PICK + 16 * PICKS + n]]
        zcom[2 * PICKS] = precv[2 * 31 + (3 + e) // 16]
        for shift in (1, 3, 2, 0):
            for n in range(4 * PICKS):
                zsend[shift, n] = precv[windows_ref[W_PICK + shift * 4 * PICKS + n]]
            for j, (src, n0, n1) in enumerate([(zsend.at[shift], 0, 4 * PICKS), (zcom, 4 * PICKS, PT)]):
                dst = zrecv.at[pl.ds(t * PT + n0, n1 - n0)]
                if shift == 0:
                    cp = pltpu.make_async_copy(src, dst, own_sem.at[1 + j])
                    cp.start()
                else:
                    cp = remote(src, dst, zp_send.at[shift - 1, j], zp_recv.at[shift - 1, j], (d, (t + shift) % NT))
                pcopies.append(cp)

    pcopies = []

    def send_heads():
        for cp in pcopies:
            cp.wait()

        def total(at):
            return zrecv[windows_ref[at]] + zrecv[windows_ref[at + 1]]

        for k in range(2):
            for i in range(2):
                bsend[k, i] = total(W_MERGE + 64 + (i * 2 + k) * 2)
            bsend[k, 2] = zrecv[3 * PT + PT - 1]
        for k in range(2):
            for m in range(8):
                for i in range(2):
                    hsend[k * 8 + m, i] = total(W_MERGE + ((2 * i + k) * 8 + m) * 2)

        @pl.loop(1, NDP)
        def _(n):
            i = (d + n) % NDP
            remote(bsend.at[i // 16], brecv.at[seq, :, e], p_send.at[1], p_recv.at[1], (i, t))

        pltpu.make_async_copy(bsend.at[d // 16], brecv.at[seq, :, e], p_recv.at[1]).start()

        @pl.loop(0, 16)
        def _(n):
            i = 16 * (n // 8) + 2 * (n % 8) + e // 8
            dst = hrecv.at[seq, :, (e // 4) % 2, e % 4]

            @pl.when(i != d)
            def _():
                remote(hsend.at[n], dst, p_send.at[2], p_recv.at[2], (i, t))

            @pl.when(i == d)
            def _():
                pltpu.make_async_copy(hsend.at[n], dst, p_recv.at[2]).start()

    high = lax.Precision.HIGHEST
    values = []

    def mix():
        await_bytes(brecv, p_recv.at[1])
        await_bytes(hrecv, p_recv.at[2])
        head = windows_ref[W_HEAD + 1]
        lower = iota((L, L), 0) <= iota((L, L), 1)
        ones = jnp.where(lower, 1.0, 0.0).astype(F32)
        qsend[...] = jnp.zeros_like(qsend)
        for s in range(2):
            bmat = brecv[s, 0].reshape(N, L)
            cmat = brecv[s, 1].reshape(N, L)
            scores = lax.dot_general(bmat, cmat, (((0,), (0,)), ((), ())), precision=high, preferred_element_type=F32)
            raw = brecv[s, 2, windows_ref[W_HEAD]]
            squares = jnp.zeros((1, L), F32)
            for hh in range(2):
                r = 2 * (d % 8) + hh
                row = jnp.sum(jnp.where(iota((TILE, L), 0) == r, raw, 0.0), axis=0, keepdims=True)
                row = row + bias_ref[head + hh]
                step = jnp.maximum(row, 0.0) + jnp.log1p(jnp.exp(-jnp.abs(row)))
                rates = jnp.broadcast_to(step * -rate_ref[head + hh], (8, L))
                cumul = jnp.dot(rates, ones, precision=high, preferred_element_type=F32)
                across = jnp.broadcast_to(cumul[0:1], (L, L))
                diff = across - across.T
                decay = jnp.where(lower, jnp.exp(jnp.where(lower, diff, 0.0)), 0.0)
                weights = scores * decay * jnp.broadcast_to(step, (L, L)).T
                xt = hrecv[s, 1, hh].reshape(P_SIZE, L)
                zt = hrecv[s, 0, hh].reshape(P_SIZE, L)
                out = jnp.dot(xt, weights, precision=high, preferred_element_type=F32) + skip_ref[head + hh] * xt
                v = out * (zt * jax.nn.sigmoid(zt))
                squares = squares + jnp.sum(v * v, axis=0, keepdims=True)
                values.append(v)
            qsend[s : s + 1] = squares
        base = 16 * (d // 16)

        @pl.loop(1, 16)
        def _(n):
            i = base + (d + n) % 16
            remote(qsend, qrecv.at[d % 16], p_send.at[3], p_recv.at[3], (i, t))

        pltpu.make_async_copy(qsend, qrecv.at[d % 16], p_recv.at[3]).start()

    def finish():
        await_bytes(qrecv, p_recv.at[3])
        total = jnp.sum(qrecv[...], axis=0)
        scale = lax.rsqrt(total / (32 * P_SIZE) + 1e-05)
        gain = gain_ref[windows_ref[W_HEAD + 2]]
        for s in range(2):
            v = jnp.concatenate(values[2 * s : 2 * s + 2], axis=0) * scale[s : s + 1]
            mixed_ref[s * L : (s + 1) * L] = (v.T * gain).astype(BF16)

    zero = jnp.zeros((TILE, L), F32)
    precv[ZERO2] = zero
    zrecv[ZERO3] = zero
    shift_part(0)
    send_part(0)
    gather_first()
    shift_part(1)
    send_part(1)
    shift_part(2)
    shift_part(3)
    gather_second()
    forward_part(0)
    send_part(2)
    gather_third()
    multiply()
    send_products()
    forward_part(1)
    send_part(3)
    forward_products()
    forward_part(2)
    send_heads()
    forward_part(3)
    forward_dt()
    mix()
    finish()

    for cp in copies:
        cp.wait()
    for p in range(NP):
        await_bytes(shifted[p].at[:, :, 0 : (NDP - 1) * F], dp_send.at[p])
    await_bytes(hid.at[0:3, 0, 0, 0:L], ag_send.at[0])
    await_bytes(hid.at[0:3, 0, 0, L:], ag_send.at[1])
    await_bytes(hid.at[0:3, :, 0, 0:L], ag_send.at[2])
    await_bytes(hid.at[0:3, :, 0, L:], ag_send.at[3])
    await_bytes(hid.at[:, :, 0], ag_send.at[4])
    await_bytes(precv.at[0 : 2 * (NDP - 1)], p_send.at[0])
    await_bytes(brecv.at[0, :, 0:16], p_send.at[1])
    await_bytes(brecv.at[1, :, 0:15], p_send.at[1])
    itself = seq == e // 8

    @pl.when(itself)
    def _():
        await_bytes(hsend.at[0:15], p_send.at[2])

    @pl.when(jnp.logical_not(itself))
    def _():
        await_bytes(hsend, p_send.at[2])

    await_bytes(qrecv.at[0:15], p_send.at[3])


def exchange(windows, rate, bias, skip, gain, hidden, flat):
    any_ = pl.BlockSpec(memory_space=pl.ANY)
    smem = pl.BlockSpec(memory_space=pltpu.SMEM)
    vmem = pl.BlockSpec(memory_space=pltpu.VMEM)
    dma = pltpu.SemaphoreType.DMA
    return pl.pallas_call(
        exchange_kernel,
        out_shape=(
            jax.ShapeDtypeStruct((NT, 6, SLOT, TILE, F), BF16),
            jax.ShapeDtypeStruct((NT, 4, TILE, F), BF16),
            jax.ShapeDtypeStruct((2 * L, L), BF16),
        ),
        in_specs=[smem, smem, smem, smem, vmem, vmem, vmem],
        out_specs=(any_, any_, vmem),
        scratch_shapes=[pltpu.VMEM((w, TILE, D), BF16) for w in PARTS]
        + [pltpu.VMEM((NDP * w, TILE, F), BF16) for w in PARTS]
        + [pltpu.VMEM((NT, 4, c, TILE, F), BF16) for c in CAPS]
        + [pltpu.VMEM((2, c, TILE, F), BF16) for c in CAPS]
        + [
            pltpu.VMEM((16, TILE, F), BF16),
            pltpu.VMEM((NT, 4, TILE, F), BF16),
            dma((NP,)),
            dma((NP,)),
            dma((NT - 1, 2 * NP + 1)),
            dma((NT - 1, 2 * NP + 1)),
            dma((2 * NP + 1,)),
            pltpu.VMEM((4, 4, 2, 2 * L, F), BF16),
            pltpu.VMEM((2, 32, TILE, L), F32),
            pltpu.VMEM((ZERO2 + 1, TILE, L), F32),
            pltpu.VMEM((NT, 4 * PICKS, TILE, L), F32),
            pltpu.VMEM((2 * PICKS + 1, TILE, L), F32),
            pltpu.VMEM((ZERO3 + 1, TILE, L), F32),
            pltpu.VMEM((16, 2, TILE, L), F32),
            pltpu.VMEM((2, 2, 2, 4, TILE, L), F32),
            pltpu.VMEM((2, 3, TILE, L), F32),
            pltpu.VMEM((2, 3, 16, TILE, L), F32),
            pltpu.VMEM((8, L), F32),
            pltpu.VMEM((16, 8, L), F32),
            dma((5,)),
            dma((5,)),
            dma((4,)),
            dma((4,)),
            dma((NT - 1, 2)),
            dma((NT - 1, 2)),
            dma((3,)),
        ],
        compiler_params=pltpu.CompilerParams(
            collective_id=1, has_side_effects=True, vmem_limit_bytes=56 << 20
        ),
        name="exchange",
    )(windows, rate, bias, skip, gain, hidden, flat)


WIDE = 1024


def place_kernel(off_ref, own_ref, place_ref, got_ref, dt_ref, out_ref, rows_ref):
    step = pl.program_id(0)
    g = owner_groups(own_ref, lax.axis_index("tensor"))
    eye = jnp.where(
        lax.broadcasted_iota(jnp.int32, (F, F), 0) == lax.broadcasted_iota(jnp.int32, (F, F), 1), 1.0, 0.0
    ).astype(BF16)

    def tile(slot, block, tau):
        at = (block * BT + tau) * 2
        one, two = place_ref[at], place_ref[at + 1]
        base = slot * SLOT
        first = got_ref[one + base]
        second = got_ref[jnp.maximum(two, 0) + base]
        return first + jnp.where(two >= 0, second, jnp.zeros_like(second))

    def emit(width):
        out_ref[:, :width] = lax.dot_general(
            eye, rows_ref[:width], (((1,), (1,)), ((), ())), preferred_element_type=F32
        ).astype(BF16)

    @pl.when(step < 8)
    def _():
        k = step // 4
        gk = jnp.where(k == 0, g[0], g[1])
        for seg in range(2):
            block = off_ref[seg] // 2048 + gk
            for j in range(8):
                u = (step % 4) * 8 + j
                for q in range(4):
                    r = j * 128 + seg * 64 + q * TILE
                    rows_ref[r : r + TILE] = tile(2 * seg + k, block, 4 * u + q)
        emit(WIDE)

    @pl.when(step == 8)
    def _():
        for seg in range(2):
            block = off_ref[2 + seg] // 2048
            for k in range(2):
                for q in range(16):
                    r = (seg * 2 + k) * 256 + q * TILE
                    rows_ref[r : r + TILE] = tile(4 + seg, block, g[k] * 16 + q)
        emit(WIDE)

    @pl.when(step == 9)
    def _():
        for j in range(4):
            rows_ref[j * TILE : (j + 1) * TILE] = dt_ref[3, j]
        emit(128)


def place(offsets, group_owner, got, dt):
    smem = pl.BlockSpec(memory_space=pltpu.SMEM)
    table = jnp.asarray(PLACE.reshape(-1))
    got = got.reshape(NT * 6 * SLOT, TILE, F)
    return pl.pallas_call(
        place_kernel,
        grid=(10,),
        out_shape=jax.ShapeDtypeStruct((F, 9280), BF16),
        in_specs=[
            smem,
            smem,
            smem,
            pl.BlockSpec((NT * 6 * SLOT, TILE, F), lambda i: (0, 0, 0)),
            pl.BlockSpec((NT, 4, TILE, F), lambda i: (0, 0, 0, 0)),
        ],
        out_specs=pl.BlockSpec((F, WIDE), lambda i: (0, i)),
        scratch_shapes=[pltpu.VMEM((WIDE, F), BF16)],
        compiler_params=pltpu.CompilerParams(vmem_limit_bytes=48 << 20),
        name="place",
    )(offsets, group_owner, table, got, dt)


def shards(flat_weight, offsets, group_owner, hidden, decay_rate, dt_bias, skip_gain, norm_gain):
    windows = prep(offsets, group_owner)
    gain = norm_gain.reshape(H // 2, 1, 2 * P_SIZE)
    got, dt_rows, mixed = exchange(windows, decay_rate, dt_bias, skip_gain, gain, hidden, flat_weight)
    return place(offsets, group_owner, got, dt_rows), mixed


def solution(mesh):
    placed = (P(("dp", "tensor"), None), P(), P(), P(None, "dp"), P(), P(), P(), P())
    return jax.shard_map(
        shards,
        mesh=mesh,
        in_specs=placed,
        out_specs=(P("dp", "tensor"), P(None, ("dp", "tensor"))),
        check_vma=False,
    )
```

time: 339 us -> 167 us (0.49)
  waiting for transfers between devices: 108 us -> 0 us
  blocking collectives: 63.1 us -> 0 us
  Pallas kernels: 122 us -> 155 us
  between operations: 15 us -> 0.72 us
  matrix products: 6.78 us -> 0 us
  local copies, waits for them, and re-layouts: 17.9 us -> 11.3 us
    psum x1 -> x0, waiting for transfers between devices: 108 us -> none  [shards(): summed = lax.psum(proj, 'dp')]
    psum x1 -> x0, blocking collectives: 63.1 us -> none  [shards(): totals = lax.psum(squares * onehot, 'dp')]
    pallas_call x1, Pallas kernels: 112 us -> 143 us  [exchange(): pl.pallas_call(exchange_kernel, out_shape=(jax.ShapeDtypeStruct((NT, 6, S...]
    dot_general x3 -> x0, matrix products: 6.78 us -> none  [the longest x1 5.12 us: shards(): proj = jnp.dot(hidden, w_local, preferred_element_type=jnp.float32)]
    unnamed x23 -> x14, local copies, waits for them, and re-layouts: 11.6 us -> 11.3 us
  transfers between devices with their start and end apart: 1 -> 0, of which waited for: 1 -> 0; matrix products, arithmetic and copies ran while one was open for 4% -> 0% of each run, Pallas kernels for 0% -> 0%
where the time goes in v2:
time: 167 us
  Pallas kernels  155 us (93%)
  local copies, waits for them, and re-layouts  11.3 us (7%)
    pallas_call x1, Pallas kernels, exchange(): pl.pallas_call(exchange_kernel, out_shape=(jax.ShapeDtypeStruct((NT, 6, S...  143 us
    unnamed x14, local copies, waits for them, and re-layouts  11.3 us
    pallas_call x1, Pallas kernels, place(): pl.pallas_call(place_kernel, grid=(10,), out_shape=jax.ShapeDtypeStruct((...  9.24 us

profile of v2, /device:TPU:1, one launch (start us, length us, event | category | flops | bytes accessed | tf_op | source)
XLA Modules:
  0.0 167.0 jit_solution(17224077811300662084)
XLA Ops:
  0.6 0.0 copy-start.2
  0.6 0.0 copy-start.4
  0.7 0.0 copy-start.3
  0.7 2.3 %prep.1.windows_ref = s32[209]{0:T(256)} custom-call(s32[5]{0:T(128)} %off_ref.3, s32[8]{0:T(128)} %own_ref.3, s32[288]{0:T(512)} %constant.8.clone.start_ref, s32[3456]{0:T(1024)} %constant.9.clone.pick_ref, s32[4608]{0:T(1024)} %constant.10.clone.merge_ref), custom_call_target="tpu_custom_call" | custom-call | tf_op jit(solution)/shard_map/prep/pallas_call | solution.py:172
  3.0 143.4 %exchange.1 = (bf16[4,6,38,16,256]{4,3,2,1,0:T(8,128)(2,1)}, bf16[4,4,16,256]{3,2,1,0:T(8,128)(2,1)}, bf16[256,128]{1,0:T(8,128)(2,1)}) custom-call(s32[209]{0:T(256)} %prep.1.windows_ref, f32[256]{0:T(256)} %rate_ref.1, f32[256]{0:T(256)} %bias_ref.1, f32[256]{0:T(256)} %skip_ref.1, f32[128,1,128]{2,1,0:T(1,128)} %bitcast.3, bf16[256,256]{1,0:T(8,128)(2,1)} %hidden_ref.1, ...), custom_call_target="tpu_custom_call" | custom-call | tf_op jit(solution)/shard_map/exchange/pallas_call | solution.py:533
  146.4 0.0 copy-done.2
  146.4 0.0 copy-done.4
  146.4 0.0 copy-done.3
  146.4 0.0 copy-start.1
  146.5 0.9 copy-done.1
  147.4 9.2 %place.1 = bf16[256,9280]{1,0:T(8,128)(2,1)S(1)} custom-call(s32[5]{0:T(128)S(1)} %copy-done.3, s32[8]{0:T(128)S(1)} %copy-done.4, s32[4608]{0:T(1024)S(1)} %copy-done.2, bf16[912,16,256]{2,1,0:T(8,128)(2,1)} %bitcast.2, bf16[4,4,16,256]{3,2,1,0:T(8,128)(2,1)S(1)} %copy-done.1), custom_call_target="tpu_custom_call" | custom-call | tf_op jit(solution)/shard_map/place/pallas_call | solution.py:638
  156.6 0.0 copy-start
  156.6 2.2 %copy-done = bf16[256,9280]{1,0:T(8,128)(2,1)} copy-done((bf16[256,9280]{1,0:T(8,128)(2,1)}, bf16[256,9280]{1,0:T(8,128)(2,1)S(1)}, u32[]{:S(2)}) %copy-start) | copy-done | bytes 4751384
  158.8 0.0 copy-start.5
  158.8 7.6 %copy.14 = bf16[256,9280]{0,1:T(8,128)(2,1)} copy(bf16[256,9280]{1,0:T(8,128)(2,1)} %copy-done) | data formatting | bytes 9502720
  166.4 0.0 copy-done.5
  166.4 0.6 copy.16
Async XLA Ops:
  0.6 145.8 %copy-start.2 = (s32[4608]{0:T(1024)S(1)}, s32[4608]{0:T(1024)}, u32[]{:S(2)}) copy-start(s32[4608]{0:T(1024)} %constant.11.clone.place_ref) | copy-start | bytes 55300
  0.6 145.8 %copy-start.4 = (s32[8]{0:T(128)S(1)}, s32[8]{0:T(128)}, u32[]{:S(2)}) copy-start(s32[8]{0:T(128)} %own_ref.3) | copy-start | bytes 100
  0.7 145.8 %copy-start.3 = (s32[5]{0:T(128)S(1)}, s32[5]{0:T(128)}, u32[]{:S(2)}) copy-start(s32[5]{0:T(128)} %off_ref.3) | copy-start | bytes 64
  146.4 0.9 copy-start.1
  156.6 2.2 %copy-start = (bf16[256,9280]{1,0:T(8,128)(2,1)}, bf16[256,9280]{1,0:T(8,128)(2,1)S(1)}, u32[]{:S(2)}) copy-start(bf16[256,9280]{1,0:T(8,128)(2,1)S(1)} %place.1) | copy-start | bytes 14254084
  158.8 7.6 %copy-start.5 = (bf16[256,128]{1,0:T(8,128)(2,1)S(1)}, bf16[256,128]{1,0:T(8,128)(2,1)}, u32[]{:S(2)}) copy-start(bf16[256,128]{1,0:T(8,128)(2,1)} %get-tuple-element.13) | copy-start | bytes 196612

commit v3 on v2

--- a/solution.py
+++ b/solution.py
@@ -477,25 +477,25 @@
     zero = jnp.zeros((TILE, L), F32)
     precv[ZERO2] = zero
     zrecv[ZERO3] = zero
+    gather_first()
     shift_part(0)
     send_part(0)
-    gather_first()
+    gather_second()
     shift_part(1)
     send_part(1)
     shift_part(2)
     shift_part(3)
-    gather_second()
+    send_part(2)
     forward_part(0)
-    send_part(2)
     gather_third()
+    send_part(3)
+    forward_part(1)
     multiply()
     send_products()
-    forward_part(1)
-    send_part(3)
+    forward_part(2)
     forward_products()
-    forward_part(2)
+    forward_part(3)
     send_heads()
-    forward_part(3)
     forward_dt()
     mix()
     finish()
@@ -533,12 +533,12 @@
     return pl.pallas_call(
         exchange_kernel,
         out_shape=(
-            jax.ShapeDtypeStruct((NT, 6, SLOT, TILE, F), BF16),
-            jax.ShapeDtypeStruct((NT, 4, TILE, F), BF16),
+            pltpu.VMEM((NT, 6, SLOT, TILE, F), BF16),
+            pltpu.VMEM((NT, 4, TILE, F), BF16),
             jax.ShapeDtypeStruct((2 * L, L), BF16),
         ),
         in_specs=[smem, smem, smem, smem, vmem, vmem, vmem],
-        out_specs=(any_, any_, vmem),
+        out_specs=(vmem, vmem, vmem),
         scratch_shapes=[pltpu.VMEM((w, TILE, D), BF16) for w in PARTS]
         + [pltpu.VMEM((NDP * w, TILE, F), BF16) for w in PARTS]
         + [pltpu.VMEM((NT, 4, c, TILE, F), BF16) for c in CAPS]
@@ -572,21 +572,18 @@
             dma((3,)),
         ],
         compiler_params=pltpu.CompilerParams(
-            collective_id=1, has_side_effects=True, vmem_limit_bytes=56 << 20
+            collective_id=1, has_side_effects=True, vmem_limit_bytes=44 << 20
         ),
         name="exchange",
     )(windows, rate, bias, skip, gain, hidden, flat)
 
 
-WIDE = 1024
-
-
-def place_kernel(off_ref, own_ref, place_ref, got_ref, dt_ref, out_ref, rows_ref):
+STEP = 64
+
+
+def place_kernel(off_ref, own_ref, place_ref, got_ref, dt_ref, out_ref):
     step = pl.program_id(0)
     g = owner_groups(own_ref, lax.axis_index("tensor"))
-    eye = jnp.where(
-        lax.broadcasted_iota(jnp.int32, (F, F), 0) == lax.broadcasted_iota(jnp.int32, (F, F), 1), 1.0, 0.0
-    ).astype(BF16)
 
     def tile(slot, block, tau):
         at = (block * BT + tau) * 2
@@ -596,11 +593,6 @@
         second = got_ref[jnp.maximum(two, 0) + base]
         return first + jnp.where(two >= 0, second, jnp.zeros_like(second))
 
-    def emit(width):
-        out_ref[:, :width] = lax.dot_general(
-            eye, rows_ref[:width], (((1,), (1,)), ((), ())), preferred_element_type=F32
-        ).astype(BF16)
-
     @pl.when(step < 8)
     def _():
         k = step // 4
@@ -608,11 +600,8 @@
         for seg in range(2):
             block = off_ref[seg] // 2048 + gk
             for j in range(8):
-                u = (step % 4) * 8 + j
                 for q in range(4):
-                    r = j * 128 + seg * 64 + q * TILE
-                    rows_ref[r : r + TILE] = tile(2 * seg + k, block, 4 * u + q)
-        emit(WIDE)
+                    out_ref[j * 8 + seg * 4 + q] = tile(2 * seg + k, block, (step % 4) * 32 + 4 * j + q)
 
     @pl.when(step == 8)
     def _():
@@ -620,37 +609,34 @@
             block = off_ref[2 + seg] // 2048
             for k in range(2):
                 for q in range(16):
-                    r = (seg * 2 + k) * 256 + q * TILE
-                    rows_ref[r : r + TILE] = tile(4 + seg, block, g[k] * 16 + q)
-        emit(WIDE)
+                    out_ref[(seg * 2 + k) * 16 + q] = tile(4 + seg, block, g[k] * 16 + q)
 
     @pl.when(step == 9)
     def _():
         for j in range(4):
-            rows_ref[j * TILE : (j + 1) * TILE] = dt_ref[3, j]
-        emit(128)
+            out_ref[j] = dt_ref[3, j]
 
 
 def place(offsets, group_owner, got, dt):
     smem = pl.BlockSpec(memory_space=pltpu.SMEM)
     table = jnp.asarray(PLACE.reshape(-1))
     got = got.reshape(NT * 6 * SLOT, TILE, F)
-    return pl.pallas_call(
+    rows = pl.pallas_call(
         place_kernel,
         grid=(10,),
-        out_shape=jax.ShapeDtypeStruct((F, 9280), BF16),
+        out_shape=jax.ShapeDtypeStruct((580, TILE, F), BF16),
         in_specs=[
             smem,
             smem,
             smem,
-            pl.BlockSpec((NT * 6 * SLOT, TILE, F), lambda i: (0, 0, 0)),
-            pl.BlockSpec((NT, 4, TILE, F), lambda i: (0, 0, 0, 0)),
+            pl.BlockSpec(memory_space=pltpu.VMEM),
+            pl.BlockSpec(memory_space=pltpu.VMEM),
         ],
-        out_specs=pl.BlockSpec((F, WIDE), lambda i: (0, i)),
-        scratch_shapes=[pltpu.VMEM((WIDE, F), BF16)],
-        compiler_params=pltpu.CompilerParams(vmem_limit_bytes=48 << 20),
+        out_specs=pl.BlockSpec((STEP, TILE, F), lambda i: (i, 0, 0)),
+        compiler_params=pltpu.CompilerParams(vmem_limit_bytes=16 << 20),
         name="place",
     )(offsets, group_owner, table, got, dt)
+    return rows.reshape(580 * TILE, F).T
 
 
 def shards(flat_weight, offsets, group_owner, hidden, decay_rate, dt_bias, skip_gain, norm_gain):

time: 167 us -> 144 us (0.86)
  Pallas kernels: 155 us -> 138 us
  local copies, waits for them, and re-layouts: 11.3 us -> 5.1 us
    pallas_call x1, Pallas kernels: 143 us -> 129 us  [exchange(): pl.pallas_call(exchange_kernel, out_shape=(pltpu.VMEM((NT, 6, SLOT, TILE,...]
    unnamed x14 -> x19, local copies, waits for them, and re-layouts: 11.3 us -> 5.1 us
    pallas_call x1, Pallas kernels: 9.24 us -> 6.59 us  [place(): pl.pallas_call(place_kernel, grid=(10,), out_shape=jax.ShapeDtypeStruct((...]
where the time goes in v3:
time: 144 us
  Pallas kernels  138 us (96%)
  local copies, waits for them, and re-layouts  5.1 us (4%)
    pallas_call x1, Pallas kernels, exchange(): pl.pallas_call(exchange_kernel, out_shape=(pltpu.VMEM((NT, 6, SLOT, TILE,...  129 us
    pallas_call x1, Pallas kernels, place(): pl.pallas_call(place_kernel, grid=(10,), out_shape=jax.ShapeDtypeStruct((...  6.59 us
    unnamed x19, local copies, waits for them, and re-layouts  5.1 us

profile of v3, /device:TPU:1, one launch (start us, length us, event | category | flops | bytes accessed | tf_op | source)
XLA Modules:
  0.0 143.7 jit_solution(7161774610526659371)
XLA Ops:
  0.6 0.0 copy-start.2
  0.6 0.0 copy-start.5
  0.7 0.0 copy-start.4
  0.7 2.3 %prep.1.windows_ref = s32[209]{0:T(256)} custom-call(s32[5]{0:T(128)} %off_ref.3, s32[8]{0:T(128)} %own_ref.3, s32[288]{0:T(512)} %constant.8.clone.start_ref, s32[3456]{0:T(1024)} %constant.9.clone.pick_ref, s32[4608]{0:T(1024)} %constant.10.clone.merge_ref), custom_call_target="tpu_custom_call" | custom-call | tf_op jit(solution)/shard_map/prep/pallas_call | solution.py:172
  3.0 0.0 copy-start
  3.0 0.9 copy-done
  3.9 0.0 copy-start.1
  3.9 0.8 copy-done.1
  4.7 0.0 copy-start.3
  4.7 0.7 copy-done.3
  5.4 0.0 copy-start.6
  5.4 0.7 copy-done.6
  6.1 0.0 copy-start.7
  6.1 0.7 copy-done.7
  6.8 0.0 copy-start.8
  6.8 0.7 copy-done.8
  7.4 129.0 %exchange.1 = (bf16[4,6,38,16,256]{4,3,2,1,0:T(8,128)(2,1)S(1)}, bf16[4,4,16,256]{3,2,1,0:T(8,128)(2,1)S(1)}, bf16[256,128]{1,0:T(8,128)(2,1)S(1)}) custom-call(s32[209]{0:T(256)S(1)} %copy-done.3, f32[256]{0:T(256)S(1)} %copy-done.6, f32[256]{0:T(256)S(1)} %copy-done.7, f32[256]{0:T(256)S(1)} %copy-done.8, f32[128,1,128]{2,1,0:T(1,128)S(1)} %bitcast.6, ...), custom_call_target="tpu_custom_call" | custom-call | tf_op jit(solution)/shard_map/exchange/pallas_call | solution.py:533
  136.5 0.0 copy-done.2
  136.5 0.0 copy-done.5
  136.5 0.0 copy-done.4
  136.5 6.6 %place.1 = bf16[580,16,256]{2,1,0:T(8,128)(2,1)} custom-call(s32[5]{0:T(128)S(1)} %copy-done.4, s32[8]{0:T(128)S(1)} %copy-done.5, s32[4608]{0:T(1024)S(1)} %copy-done.2, bf16[912,16,256]{2,1,0:T(8,128)(2,1)S(1)} %bitcast.5, bf16[4,4,16,256]{3,2,1,0:T(8,128)(2,1)S(1)} %get-tuple-element.6.dt_ref), custom_call_target="tpu_custom_call" | custom-call | tf_op jit(solution)/shard_map/place/pallas_call | solution.py:624
  143.1 0.6 copy.15
Async XLA Ops:
  0.6 135.8 %copy-start.2 = (s32[4608]{0:T(1024)S(1)}, s32[4608]{0:T(1024)}, u32[]{:S(2)}) copy-start(s32[4608]{0:T(1024)} %constant.11.clone.place_ref) | copy-start | bytes 55300
  0.6 135.8 %copy-start.5 = (s32[8]{0:T(128)S(1)}, s32[8]{0:T(128)}, u32[]{:S(2)}) copy-start(s32[8]{0:T(128)} %own_ref.3) | copy-start | bytes 100
  0.7 135.8 %copy-start.4 = (s32[5]{0:T(128)S(1)}, s32[5]{0:T(128)}, u32[]{:S(2)}) copy-start(s32[5]{0:T(128)} %off_ref.3) | copy-start | bytes 64
  3.0 0.9 copy-start
  3.9 0.8 copy-start.1
  4.7 0.7 copy-start.3
  5.4 0.7 copy-start.6
  6.1 0.7 copy-start.7
  6.8 0.7 copy-start.8

commit v4 on v3

--- a/solution.py
+++ b/solution.py
@@ -22,8 +22,9 @@
 CHUNK = 19
 BLOCKS = 18
 BT = 128
-PARTS = (4, 5, 5, 5)
-STARTS = (0, 4, 9, 14)
+PARTS = (6, 5, 5, 3)
+STARTS = (0, 6, 11, 16)
+COMMON = (0, 1, 8, 9, 16, 17)
 MESH = pl.DeviceIdType.MESH
 BF16 = jnp.bfloat16
 F32 = jnp.float32
@@ -57,8 +58,21 @@
     place = np.full((BLOCKS, BT, 2), -1, np.int32)
     for (b, tau), found in where.items():
         for e, (t, p, i) in enumerate(found):
-            place[b, tau, e] = t * 6 * slot + offs[p] + i - start[p, t, b]
-    return caps, [int(o) for o in offs], slot, start, place
+            place[b, tau, e] = t * 4 * slot + offs[p] + i - start[p, t, b]
+    spread = {}
+    for (b, tau), found in sorted(where.items()):
+        for t, p, i in found:
+            if b in COMMON:
+                spread.setdefault((t, b, tau % 4), []).append((tau, offs[p] + i - start[p, t, b]))
+    width = max(len(v) for v in spread.values())
+    relay = np.full((NT, BLOCKS, 4, width), -1, np.int32)
+    gathered = np.full((4, BLOCKS, 32, 2), -1, np.int32)
+    for (t, b, r), found in spread.items():
+        for n, (tau, at) in enumerate(found):
+            relay[t, b, r, n] = at
+            e = int(gathered[r, b, tau // 4, 0] >= 0)
+            gathered[r, b, tau // 4, e] = t * 2 * width + n
+    return caps, [int(o) for o in offs], slot, start, place, width, relay, gathered
 
 
 PICKS = 3
@@ -87,14 +101,18 @@
     return pick, merge
 
 
-CAPS, OFFS, SLOT, START, PLACE = make_tables()
+CAPS, OFFS, SLOT, START, PLACE, WIDTH, RELAY, GATHERED = make_tables()
 PICK, MERGE = make_product_tables()
 NP = len(PARTS)
 W_DT = NP * 18
 W_PICK = W_DT + 8
 W_MERGE = W_PICK + 18 * PICKS
 W_HEAD = W_MERGE + 72
-W_SIZE = W_HEAD + 3
+W_RELAY = W_HEAD + 3
+W_GATHER = W_RELAY + 8 * WIDTH
+W_SIZE = W_GATHER + NT * 32
+ZERO_B = 2 * SLOT
+ZERO_R = NT * 2 * WIDTH
 
 
 def dp_order():
@@ -125,7 +143,9 @@
     return jnp.clip(first, 0, G - 1), jnp.clip(last, 0, G - 1)
 
 
-def prep_kernel(off_ref, own_ref, start_ref, pick_ref, merge_ref, windows_ref):
+def find_windows(
+    off_ref, own_ref, start_ref, pick_ref, merge_ref, relay_ref, gathered_ref, windows_ref
+):
     d = lax.axis_index("dp")
     t = lax.axis_index("tensor")
     e = d // 2
@@ -165,39 +185,76 @@
     windows_ref[W_HEAD] = 2 * mine + (d % 16) // 8
     windows_ref[W_HEAD + 1] = 32 * mine + 2 * (d % 16)
     windows_ref[W_HEAD + 2] = 16 * mine + d % 16
-
-
-def prep(offsets, group_owner):
-    smem = pl.BlockSpec(memory_space=pltpu.SMEM)
-    return pl.pallas_call(
-        prep_kernel,
-        out_shape=jax.ShapeDtypeStruct((W_SIZE,), jnp.int32),
-        in_specs=[smem] * 5,
-        out_specs=smem,
-        name="prep",
-    )(
-        offsets,
-        group_owner,
-        jnp.asarray(START.reshape(-1)),
-        jnp.asarray(PICK.reshape(-1)),
-        jnp.asarray(MERGE.reshape(-1)),
-    )
+    for shift in range(NT):
+        g = owner_groups(own_ref, (t + shift) % NT)
+        for i in range(2):
+            for n in range(WIDTH):
+                v = relay_ref[((t * BLOCKS + seg[2 + i]) * 4 + (t + shift) % NT) * WIDTH + n]
+                windows_ref[W_RELAY + (shift * 2 + i) * WIDTH + n] = jnp.where(v < 0, ZERO_B, v + i * SLOT)
+            for k in range(2):
+                for u in range(4):
+                    for n in range(2):
+                        v = gathered_ref[((t * BLOCKS + seg[2 + i]) * 32 + g[k] * 4 + u) * 2 + n]
+                        at = W_GATHER + shift * 32 + ((i * 2 + k) * 4 + u) * 2 + n
+                        windows_ref[at] = jnp.where(v < 0, ZERO_R, v + i * WIDTH)
 
 
 def iota(shape, dim):
     return lax.broadcasted_iota(jnp.int32, shape, dim)
 
 
+class Table:
+    def __init__(self, ref, base):
+        self.ref, self.base = ref, base
+
+    def __getitem__(self, i):
+        return self.ref[self.base + i]
+
+
+TABLES = np.concatenate([a.reshape(-1) for a in (START, PICK, MERGE, RELAY, GATHERED)])
+BASES = np.cumsum([0, START.size, PICK.size, MERGE.size, RELAY.size])
+
+
 def exchange_kernel(
-    windows_ref, rate_ref, bias_ref, skip_ref, gain_ref, hidden_ref, flat_ref, out_ref, dt_ref, mixed_ref, *scratch
+    off_hbm,
+    own_hbm,
+    table_hbm,
+    rate_hbm,
+    bias_hbm,
+    skip_hbm,
+    gain_hbm,
+    hidden_ref,
+    flat_hbm,
+    out_ref,
+    bc_ref,
+    dt_ref,
+    mixed_ref,
+    windows_ref,
+    *scratch,
 ):
+    loads = scratch[-9:]
+    scratch = scratch[:-9]
+    off_ref, own_ref, table_ref, rate_ref, bias_ref, skip_ref, gain_ref, flat_ref, load_sem = loads
+    whole = [
+        (flat_hbm, flat_ref),
+        (off_hbm, off_ref),
+        (own_hbm, own_ref),
+        (table_hbm, table_ref),
+        (rate_hbm, rate_ref),
+        (bias_hbm, bias_ref),
+        (skip_hbm, skip_ref),
+        (gain_hbm, gain_ref),
+    ]
+    loading = [pltpu.make_async_copy(src, dst, load_sem.at[i]) for i, (src, dst) in enumerate(whole)]
+    for cp in loading:
+        cp.start()
     shifted = scratch[:NP]
     recv = scratch[NP : 2 * NP]
     send = scratch[2 * NP : 3 * NP]
-    both = scratch[3 * NP : 4 * NP]
-    dtbuf, dtsend, dp_send, dp_recv, z_send, z_recv, self_sem = scratch[4 * NP : 4 * NP + 7]
-    hid, prod, precv, zsend, zcom, zrecv, hsend, hrecv, bsend, brecv, qsend, qrecv = scratch[4 * NP + 7 : 4 * NP + 19]
-    ag_send, ag_recv, p_send, p_recv, zp_send, zp_recv, own_sem = scratch[4 * NP + 19 :]
+    dtbuf, dtsend, dp_send, dp_recv, z_send, z_recv, self_sem = scratch[3 * NP : 3 * NP + 7]
+    hid, prod, precv, zsend, zcom, zrecv, hsend, hrecv, bsend, brecv, qsend, qrecv = scratch[3 * NP + 7 : 3 * NP + 19]
+    ag_send, ag_recv, p_send, p_recv, zp_send, zp_recv, own_sem = scratch[3 * NP + 19 : 3 * NP + 26]
+    bcbuf, spread, gather, owned, b_send, b_recv, b_self = scratch[3 * NP + 26 :]
     d = lax.axis_index("dp")
     t = lax.axis_index("tensor")
     x, y, c = d // 8, (d // 2) % 4, d % 2
@@ -260,53 +317,62 @@
     def forward_part(p):
         await_bytes(recv[p], dp_recv.at[p])
 
-        def pack(dst, window):
+        def pack(dst, window, at=0):
             first = windows_ref[window]
 
             @pl.loop(0, CAPS[p], unroll=2)
             def _(j):
-                dst[j] = recv[p][first + j]
+                dst[at + j] = recv[p][first + j]
 
         for i in range(2):
-            pack(both[p].at[i], p * 18 + 16 + i)
+            pack(bcbuf, p * 18 + 16 + i, i * SLOT + OFFS[p])
         for l in range(max(STARTS[p], 3), STARTS[p] + PARTS[p]):
             dtbuf[l - 3] = recv[p][31 * PARTS[p] + l - STARTS[p]]
+        if p == NP - 1:
+            spread_common()
         for shift in (1, 3, 2, 0):
             for s in range(4):
                 pack(send[p].at[shift, s], p * 18 + shift * 4 + s)
-            span = pl.ds(OFFS[p], CAPS[p])
-            pairs = [(send[p].at[shift], out_ref.at[t, 0:4, span]), (both[p], out_ref.at[t, 4:6, span])]
-            for n, (src, dst) in enumerate(pairs):
-                if shift == 0:
-                    cp = pltpu.make_async_copy(src, dst, self_sem.at[2 * p + n])
-                    cp.start()
-                else:
-                    cp = remote(
-                        src,
-                        dst,
-                        z_send.at[shift - 1, 2 * p + n],
-                        z_recv.at[shift - 1, 2 * p + n],
-                        (d, (t + shift) % NT),
-                    )
-                copies.append(cp)
+            src, dst = send[p].at[shift], out_ref.at[t, :, pl.ds(OFFS[p], CAPS[p])]
+            to_owner(src, dst, shift, p)
+
+    def to_owner(src, dst, shift, n):
+        if shift == 0:
+            cp = pltpu.make_async_copy(src, dst, self_sem.at[n])
+            cp.start()
+        else:
+            cp = remote(src, dst, z_send.at[shift - 1, n], z_recv.at[shift - 1, n], (d, (t + shift) % NT))
+        copies.append(cp)
+
+    bcopies = []
+
+    def spread_common():
+        for shift in (1, 3, 2, 0):
+            for n in range(2 * WIDTH):
+                spread[shift, n] = bcbuf[windows_ref[W_RELAY + shift * 2 * WIDTH + n]]
+            dst = gather.at[pl.ds(t * 2 * WIDTH, 2 * WIDTH)]
+            if shift == 0:
+                cp = pltpu.make_async_copy(spread.at[0], dst, b_self.at[0])
+                cp.start()
+            else:
+                cp = remote(spread.at[shift], dst, b_send.at[shift - 1], b_recv.at[shift - 1], (d, (t + shift) % NT))
+            bcopies.append(cp)
+
+    def share_common():
+        for cp in bcopies:
+            cp.wait()
+        for shift in (1, 3, 2, 0):
+            for n in range(16):
+                at = W_GATHER + shift * 32 + 2 * n
+                owned[shift, n] = gather[windows_ref[at]] + gather[windows_ref[at + 1]]
+            to_owner(owned.at[shift], bc_ref.at[t], shift, NP + 1)
 
     def forward_dt():
         for shift in (1, 3, 2, 0):
             for i in range(2):
                 for j in range(2):
                     dtsend[shift, 2 * i + j] = dtbuf[windows_ref[W_DT + shift * 2 + i] + j]
-            if shift == 0:
-                cp = pltpu.make_async_copy(dtsend.at[0], dt_ref.at[t], self_sem.at[2 * NP])
-                cp.start()
-            else:
-                cp = remote(
-                    dtsend.at[shift],
-                    dt_ref.at[t],
-                    z_send.at[shift - 1, 2 * NP],
-                    z_recv.at[shift - 1, 2 * NP],
-                    (d, (t + shift) % NT),
-                )
-            copies.append(cp)
+            to_owner(dtsend.at[shift], dt_ref.at[t], shift, NP)
 
     def along_x(i):
         return (((x + i) % 4) * 8 + y * 2 + c, t)
@@ -402,9 +468,9 @@
                 for i in range(2):
                     hsend[k * 8 + m, i] = total(W_MERGE + ((2 * i + k) * 8 + m) * 2)
 
-        @pl.loop(1, NDP)
+        @pl.loop(1, 16)
         def _(n):
-            i = (d + n) % NDP
+            i = (d + 2 * n) % NDP
             remote(bsend.at[i // 16], brecv.at[seq, :, e], p_send.at[1], p_recv.at[1], (i, t))
 
         pltpu.make_async_copy(bsend.at[d // 16], brecv.at[seq, :, e], p_recv.at[1]).start()
@@ -425,8 +491,12 @@
     high = lax.Precision.HIGHEST
     values = []
 
+    def share_products():
+        await_bytes(brecv.at[seq], p_recv.at[1])
+        remote(brecv.at[seq], brecv.at[seq], p_send.at[4], p_recv.at[4], (d + 1 - 2 * c, t))
+
     def mix():
-        await_bytes(brecv, p_recv.at[1])
+        await_bytes(brecv.at[seq], p_recv.at[4])
         await_bytes(hrecv, p_recv.at[2])
         head = windows_ref[W_HEAD + 1]
         lower = iota((L, L), 0) <= iota((L, L), 1)
@@ -475,9 +545,12 @@
             mixed_ref[s * L : (s + 1) * L] = (v.T * gain).astype(BF16)
 
     zero = jnp.zeros((TILE, L), F32)
+    bcbuf[ZERO_B] = jnp.zeros((TILE, F), BF16)
+    gather[ZERO_R] = jnp.zeros((TILE, F), BF16)
     precv[ZERO2] = zero
     zrecv[ZERO3] = zero
     gather_first()
+    loading[0].wait()
     shift_part(0)
     send_part(0)
     gather_second()
@@ -485,19 +558,24 @@
     send_part(1)
     shift_part(2)
     shift_part(3)
-    send_part(2)
+    for cp in loading[1:]:
+        cp.wait()
+    find_windows(off_ref, own_ref, *[Table(table_ref, int(i)) for i in BASES], windows_ref)
     forward_part(0)
     gather_third()
-    send_part(3)
-    forward_part(1)
     multiply()
     send_products()
+    send_part(2)
+    forward_part(1)
+    forward_products()
+    send_part(3)
     forward_part(2)
-    forward_products()
+    send_heads()
+    share_products()
     forward_part(3)
-    send_heads()
     forward_dt()
     mix()
+    share_common()
     finish()
 
     for cp in copies:
@@ -510,8 +588,8 @@
     await_bytes(hid.at[0:3, :, 0, L:], ag_send.at[3])
     await_bytes(hid.at[:, :, 0], ag_send.at[4])
     await_bytes(precv.at[0 : 2 * (NDP - 1)], p_send.at[0])
-    await_bytes(brecv.at[0, :, 0:16], p_send.at[1])
     await_bytes(brecv.at[1, :, 0:15], p_send.at[1])
+    await_bytes(brecv.at[1], p_send.at[4])
     itself = seq == e // 8
 
     @pl.when(itself)
@@ -525,32 +603,32 @@
     await_bytes(qrecv.at[0:15], p_send.at[3])
 
 
-def exchange(windows, rate, bias, skip, gain, hidden, flat):
-    any_ = pl.BlockSpec(memory_space=pl.ANY)
-    smem = pl.BlockSpec(memory_space=pltpu.SMEM)
+def exchange(offsets, owner, rate, bias, skip, gain, hidden, flat):
+    hbm = pl.BlockSpec(memory_space=pltpu.HBM)
     vmem = pl.BlockSpec(memory_space=pltpu.VMEM)
     dma = pltpu.SemaphoreType.DMA
     return pl.pallas_call(
         exchange_kernel,
         out_shape=(
-            pltpu.VMEM((NT, 6, SLOT, TILE, F), BF16),
+            pltpu.VMEM((NT, 4, SLOT, TILE, F), BF16),
+            pltpu.VMEM((NT, 16, TILE, F), BF16),
             pltpu.VMEM((NT, 4, TILE, F), BF16),
             jax.ShapeDtypeStruct((2 * L, L), BF16),
         ),
-        in_specs=[smem, smem, smem, smem, vmem, vmem, vmem],
-        out_specs=(vmem, vmem, vmem),
-        scratch_shapes=[pltpu.VMEM((w, TILE, D), BF16) for w in PARTS]
+        in_specs=[hbm] * 9,
+        out_specs=(vmem,) * 4,
+        scratch_shapes=[pltpu.SMEM((W_SIZE,), jnp.int32)]
+        + [pltpu.VMEM((w, TILE, D), BF16) for w in PARTS]
         + [pltpu.VMEM((NDP * w, TILE, F), BF16) for w in PARTS]
         + [pltpu.VMEM((NT, 4, c, TILE, F), BF16) for c in CAPS]
-        + [pltpu.VMEM((2, c, TILE, F), BF16) for c in CAPS]
         + [
             pltpu.VMEM((16, TILE, F), BF16),
             pltpu.VMEM((NT, 4, TILE, F), BF16),
             dma((NP,)),
             dma((NP,)),
-            dma((NT - 1, 2 * NP + 1)),
-            dma((NT - 1, 2 * NP + 1)),
-            dma((2 * NP + 1,)),
+            dma((NT - 1, NP + 2)),
+            dma((NT - 1, NP + 2)),
+            dma((NP + 2,)),
             pltpu.VMEM((4, 4, 2, 2 * L, F), BF16),
             pltpu.VMEM((2, 32, TILE, L), F32),
             pltpu.VMEM((ZERO2 + 1, TILE, L), F32),
@@ -565,23 +643,39 @@
             pltpu.VMEM((16, 8, L), F32),
             dma((5,)),
             dma((5,)),
-            dma((4,)),
-            dma((4,)),
+            dma((5,)),
+            dma((5,)),
             dma((NT - 1, 2)),
             dma((NT - 1, 2)),
             dma((3,)),
+            pltpu.VMEM((ZERO_B + 1, TILE, F), BF16),
+            pltpu.VMEM((NT, 2 * WIDTH, TILE, F), BF16),
+            pltpu.VMEM((ZERO_R + 1, TILE, F), BF16),
+            pltpu.VMEM((NT, 16, TILE, F), BF16),
+            dma((NT - 1,)),
+            dma((NT - 1,)),
+            dma((1,)),
+            pltpu.SMEM((5,), jnp.int32),
+            pltpu.SMEM((G,), jnp.int32),
+            pltpu.SMEM(TABLES.shape, jnp.int32),
+            pltpu.SMEM((H,), F32),
+            pltpu.SMEM((H,), F32),
+            pltpu.SMEM((H,), F32),
+            pltpu.VMEM((H // 2, 1, 2 * P_SIZE), F32),
+            pltpu.VMEM((ROWS, D), BF16),
+            dma((8,)),
         ],
         compiler_params=pltpu.CompilerParams(
-            collective_id=1, has_side_effects=True, vmem_limit_bytes=44 << 20
+            collective_id=1, has_side_effects=True, vmem_limit_bytes=58 << 20
         ),
         name="exchange",
-    )(windows, rate, bias, skip, gain, hidden, flat)
+    )(offsets, owner, jnp.asarray(TABLES), rate, bias, skip, gain, hidden, flat)
 
 
 STEP = 64
 
 
-def place_kernel(off_ref, own_ref, place_ref, got_ref, dt_ref, out_ref):
+def place_kernel(off_ref, own_ref, place_ref, got_ref, bc_ref, dt_ref, out_ref):
     step = pl.program_id(0)
     g = owner_groups(own_ref, lax.axis_index("tensor"))
 
@@ -605,11 +699,9 @@
 
     @pl.when(step == 8)
     def _():
-        for seg in range(2):
-            block = off_ref[2 + seg] // 2048
-            for k in range(2):
-                for q in range(16):
-                    out_ref[(seg * 2 + k) * 16 + q] = tile(4 + seg, block, g[k] * 16 + q)
+        for n in range(4):
+            for q in range(16):
+                out_ref[n * 16 + q] = bc_ref[q % 4, n * 4 + q // 4]
 
     @pl.when(step == 9)
     def _():
@@ -617,10 +709,10 @@
             out_ref[j] = dt_ref[3, j]
 
 
-def place(offsets, group_owner, got, dt):
+def place(offsets, group_owner, got, bc, dt):
     smem = pl.BlockSpec(memory_space=pltpu.SMEM)
     table = jnp.asarray(PLACE.reshape(-1))
-    got = got.reshape(NT * 6 * SLOT, TILE, F)
+    got = got.reshape(NT * 4 * SLOT, TILE, F)
     rows = pl.pallas_call(
         place_kernel,
         grid=(10,),
@@ -631,19 +723,21 @@
             smem,
             pl.BlockSpec(memory_space=pltpu.VMEM),
             pl.BlockSpec(memory_space=pltpu.VMEM),
+            pl.BlockSpec(memory_space=pltpu.VMEM),
         ],
         out_specs=pl.BlockSpec((STEP, TILE, F), lambda i: (i, 0, 0)),
         compiler_params=pltpu.CompilerParams(vmem_limit_bytes=16 << 20),
         name="place",
-    )(offsets, group_owner, table, got, dt)
+    )(offsets, group_owner, table, got, bc, dt)
     return rows.reshape(580 * TILE, F).T
 
 
 def shards(flat_weight, offsets, group_owner, hidden, decay_rate, dt_bias, skip_gain, norm_gain):
-    windows = prep(offsets, group_owner)
     gain = norm_gain.reshape(H // 2, 1, 2 * P_SIZE)
-    got, dt_rows, mixed = exchange(windows, decay_rate, dt_bias, skip_gain, gain, hidden, flat_weight)
-    return place(offsets, group_owner, got, dt_rows), mixed
+    got, bc, dt_rows, mixed = exchange(
+        offsets, group_owner, decay_rate, dt_bias, skip_gain, gain, hidden, flat_weight
+    )
+    return place(offsets, group_owner, got, bc, dt_rows), mixed
 
 
 def solution(mesh):

time: 144 us -> 130 us (0.903)
  Pallas kernels: 138 us -> 128 us
  local copies, waits for them, and re-layouts: 5.1 us -> 0.65 us
    pallas_call x2 -> x1, Pallas kernels: 131 us -> 122 us  [exchange(): pl.pallas_call(exchange_kernel, out_shape=(pltpu.VMEM((NT, 4, SLOT, TILE,...]
    unnamed x19 -> x9, local copies, waits for them, and re-layouts: 5.1 us -> 0.65 us
where the time goes in v4:
time: 130 us
  Pallas kernels  128 us (98%)
    pallas_call x1, Pallas kernels, exchange(): pl.pallas_call(exchange_kernel, out_shape=(pltpu.VMEM((NT, 4, SLOT, TILE,...  122 us
    pallas_call x1, Pallas kernels, place(): pl.pallas_call(place_kernel, grid=(10,), out_shape=jax.ShapeDtypeStruct((...  6.52 us

profile of v4, /device:TPU:1, one launch (start us, length us, event | category | flops | bytes accessed | tf_op | source)
XLA Modules:
  0.0 129.6 jit_solution(8731746527944880690)
XLA Ops:
  0.6 0.0 copy-start
  0.6 0.0 copy-start.2
  0.7 0.0 copy-start.1
  0.7 121.7 %exchange.1 = (bf16[4,4,38,16,256]{4,3,2,1,0:T(8,128)(2,1)S(1)}, bf16[4,16,16,256]{3,2,1,0:T(8,128)(2,1)S(1)}, bf16[4,4,16,256]{3,2,1,0:T(8,128)(2,1)S(1)}, bf16[256,128]{1,0:T(8,128)(2,1)}) custom-call(s32[5]{0:T(128)} %off_ref.1, s32[8]{0:T(128)} %own_ref.1, s32[15840]{0:T(1024)} %constant.4.clone.table_hbm, f32[256]{0:T(256)} %rate_hbm.1, f32[256]{0:T(256)} %bias_hbm.1, ...), custom_call_target="tpu_custom_call" | custom-call | tf_op jit(solution)/shard_map/exchange/pallas_call | solution.py:610
  122.4 0.0 copy-done
  122.4 0.0 copy-done.2
  122.4 0.0 copy-done.1
  122.4 0.0 copy-start.3
  122.4 6.5 %place.1 = bf16[580,16,256]{2,1,0:T(8,128)(2,1)} custom-call(s32[5]{0:T(128)S(1)} %copy-done.1, s32[8]{0:T(128)S(1)} %copy-done.2, s32[4608]{0:T(1024)S(1)} %copy-done, bf16[608,16,256]{2,1,0:T(8,128)(2,1)S(1)} %bitcast.5, bf16[4,16,16,256]{3,2,1,0:T(8,128)(2,1)S(1)} %get-tuple-element.7.bc_ref, bf16[4,4,16,256]{3,2,1,0:T(8,128)(2,1)S(1)} %get-tuple-element.8.dt_ref), custom_call_target="tpu_custom_call" | custom-call | tf_op jit(solution)/shard_map/place/pallas_call | solution.py:716
  128.9 0.0 copy-done.3
  128.9 0.6 copy.13
Async XLA Ops:
  0.6 121.7 %copy-start = (s32[4608]{0:T(1024)S(1)}, s32[4608]{0:T(1024)}, u32[]{:S(2)}) copy-start(s32[4608]{0:T(1024)} %constant.5.clone.place_ref) | copy-start | bytes 55300
  0.6 121.7 %copy-start.2 = (s32[8]{0:T(128)S(1)}, s32[8]{0:T(128)}, u32[]{:S(2)}) copy-start(s32[8]{0:T(128)} %own_ref.1) | copy-start | bytes 100
  0.7 121.7 %copy-start.1 = (s32[5]{0:T(128)S(1)}, s32[5]{0:T(128)}, u32[]{:S(2)}) copy-start(s32[5]{0:T(128)} %off_ref.1) | copy-start | bytes 64
  122.4 6.5 %copy-start.3 = (bf16[256,128]{1,0:T(8,128)(2,1)S(1)}, bf16[256,128]{1,0:T(8,128)(2,1)}, u32[]{:S(2)}) copy-start(bf16[256,128]{1,0:T(8,128)(2,1)} %get-tuple-element.13) | copy-start | bytes 196612

commit v5 on v4

--- a/solution.py
+++ b/solution.py
@@ -22,8 +22,8 @@
 CHUNK = 19
 BLOCKS = 18
 BT = 128
-PARTS = (6, 5, 5, 3)
-STARTS = (0, 6, 11, 16)
+PARTS = (4, 4, 4, 4, 3)
+STARTS = (0, 4, 8, 12, 16)
 COMMON = (0, 1, 8, 9, 16, 17)
 MESH = pl.DeviceIdType.MESH
 BF16 = jnp.bfloat16
@@ -63,16 +63,19 @@
     for (b, tau), found in sorted(where.items()):
         for t, p, i in found:
             if b in COMMON:
-                spread.setdefault((t, b, tau % 4), []).append((tau, offs[p] + i - start[p, t, b]))
-    width = max(len(v) for v in spread.values())
+                key = (t, b, tau % 4)
+                spread.setdefault(key, ([], []))[int(p == n - 1)].append((tau, offs[p] + i - start[p, t, b]))
+    early = max(len(v[0]) for v in spread.values())
+    width = early + max(len(v[1]) for v in spread.values())
     relay = np.full((NT, BLOCKS, 4, width), -1, np.int32)
     gathered = np.full((4, BLOCKS, 32, 2), -1, np.int32)
     for (t, b, r), found in spread.items():
-        for n, (tau, at) in enumerate(found):
-            relay[t, b, r, n] = at
-            e = int(gathered[r, b, tau // 4, 0] >= 0)
-            gathered[r, b, tau // 4, e] = t * 2 * width + n
-    return caps, [int(o) for o in offs], slot, start, place, width, relay, gathered
+        for m, tiles in enumerate(found):
+            for j, (tau, at) in enumerate(tiles, m * early):
+                relay[t, b, r, j] = at
+                e = int(gathered[r, b, tau // 4, 0] >= 0)
+                gathered[r, b, tau // 4, e] = t * 2 * width + j
+    return caps, [int(o) for o in offs], slot, start, place, early, width, relay, gathered
 
 
 PICKS = 3
@@ -101,9 +104,23 @@
     return pick, merge
 
 
-CAPS, OFFS, SLOT, START, PLACE, WIDTH, RELAY, GATHERED = make_tables()
+CAPS, OFFS, SLOT, START, PLACE, EARLY, WIDTH, RELAY, GATHERED = make_tables()
 PICK, MERGE = make_product_tables()
 NP = len(PARTS)
+FIXES = 2
+
+
+def make_fixes():
+    fixes = np.full((BLOCKS, 4, FIXES, 3), -1, np.int32)
+    for b in range(BLOCKS):
+        for quarter in range(4):
+            found = [q for q in range(32) if PLACE[b, quarter * 32 + q, 1] >= 0]
+            for n, q in enumerate(found):
+                fixes[b, quarter, n] = q, *PLACE[b, quarter * 32 + q]
+    return fixes
+
+
+FIX = make_fixes()
 W_DT = NP * 18
 W_PICK = W_DT + 8
 W_MERGE = W_PICK + 18 * PICKS
@@ -123,7 +140,7 @@
         for q in ((a, b, c), (b, a, c), (-a % 4, -b % 4, c), (-b % 4, -a % 4, c)):
             if q not in out:
                 out.append(q)
-    return out[::-1]
+    return out
 
 
 ORDER = dp_order()
@@ -328,8 +345,8 @@
             pack(bcbuf, p * 18 + 16 + i, i * SLOT + OFFS[p])
         for l in range(max(STARTS[p], 3), STARTS[p] + PARTS[p]):
             dtbuf[l - 3] = recv[p][31 * PARTS[p] + l - STARTS[p]]
-        if p == NP - 1:
-            spread_common()
+        if p >= NP - 2:
+            spread_common(p - (NP - 2))
         for shift in (1, 3, 2, 0):
             for s in range(4):
                 pack(send[p].at[shift, s], p * 18 + shift * 4 + s)
@@ -346,17 +363,22 @@
 
     bcopies = []
 
-    def spread_common():
+    def spread_common(late):
+        low, high = (EARLY, WIDTH) if late else (0, EARLY)
         for shift in (1, 3, 2, 0):
-            for n in range(2 * WIDTH):
-                spread[shift, n] = bcbuf[windows_ref[W_RELAY + shift * 2 * WIDTH + n]]
-            dst = gather.at[pl.ds(t * 2 * WIDTH, 2 * WIDTH)]
-            if shift == 0:
-                cp = pltpu.make_async_copy(spread.at[0], dst, b_self.at[0])
-                cp.start()
-            else:
-                cp = remote(spread.at[shift], dst, b_send.at[shift - 1], b_recv.at[shift - 1], (d, (t + shift) % NT))
-            bcopies.append(cp)
+            for i in range(2):
+                for n in range(i * WIDTH + low, i * WIDTH + high):
+                    spread[shift, n] = bcbuf[windows_ref[W_RELAY + shift * 2 * WIDTH + n]]
+                src = spread.at[shift, pl.ds(i * WIDTH + low, high - low)]
+                dst = gather.at[pl.ds((t * 2 + i) * WIDTH + low, high - low)]
+                j = 2 * late + i
+                if shift == 0:
+                    cp = pltpu.make_async_copy(src, dst, b_self.at[j])
+                    cp.start()
+                else:
+                    sems = b_send.at[shift - 1, j], b_recv.at[shift - 1, j]
+                    cp = remote(src, dst, *sems, (d, (t + shift) % NT))
+                bcopies.append(cp)
 
     def share_common():
         for cp in bcopies:
@@ -380,42 +402,63 @@
     def along_y(i):
         return (x * 8 + ((y + i) % 4) * 2 + c, t)
 
+    quarter = L // NT
+    pieces = []
+    for first, size in ((pl.multiple_of(t * quarter, TILE), quarter // 2), (L, L // 2)):
+        pieces.append((pl.ds(first, size), size, along_x, along_y))
+        pieces.append((pl.ds(first + size, size), size, along_y, along_x))
+
     def gather_first():
-        own = pltpu.make_async_copy(hidden_ref, hid.at[x, y, c], own_sem.at[0])
-        own.start()
-        for i in (1, 3, 2):
-            remote(hidden_ref.at[0:L], hid.at[x, y, c, 0:L], ag_send.at[0], ag_recv.at[0], along_x(i))
-            remote(hidden_ref.at[L:], hid.at[x, y, c, L:], ag_send.at[1], ag_recv.at[1], along_y(i))
-        own.wait()
+        owns = []
+        for n, (first, size) in enumerate(((pl.multiple_of(t * quarter, TILE), quarter), (L, L))):
+            tokens = pl.ds(first, size)
+            owns.append(pltpu.make_async_copy(hidden_ref.at[tokens], hid.at[x, y, c, tokens], own_sem.at[3 * n]))
+            owns[n].start()
+        for j, (tokens, _, partner, _) in enumerate(pieces):
+            for i in (2, 1, 3):
+                remote(hidden_ref.at[tokens], hid.at[x, y, c, tokens], ag_send.at[j], ag_recv.at[j], partner(i))
+        for cp in owns:
+            cp.wait()
 
     def gather_second():
-        await_bytes(hid.at[0:3, 0, 0, 0:L], ag_recv.at[0])
-        for i in (1, 3, 2):
-            remote(hid.at[:, y, c, 0:L], hid.at[:, y, c, 0:L], ag_send.at[2], ag_recv.at[2], along_y(i))
-        await_bytes(hid.at[0:3, 0, 0, L:], ag_recv.at[1])
-        for i in (1, 3, 2):
-            remote(hid.at[x, :, c, L:], hid.at[x, :, c, L:], ag_send.at[3], ag_recv.at[3], along_x(i))
+        for j, (tokens, size, first, then) in enumerate(pieces):
+            await_bytes(hid.at[0:3, 0, 0, 0:size], ag_recv.at[j])
+            line = hid.at[:, y, c, tokens] if first is along_x else hid.at[x, :, c, tokens]
+            for i in (2, 1, 3):
+                remote(line, line, ag_send.at[4 + j], ag_recv.at[4 + j], then(i))
+
+    def gather_planes():
+        for j in range(2):
+            await_bytes(hid.at[0:3, :, 0, 0 : pieces[j][1]], ag_recv.at[4 + j])
+        part = hid.at[:, :, c, pl.ds(pl.multiple_of(t * quarter, TILE), quarter)]
+        for i in (2, 1, 3):
+            remote(part, part, ag_send.at[8], ag_recv.at[8], (d, (t + i) % NT))
 
     def gather_third():
-        await_bytes(hid.at[0:3, :, 0, 0:L], ag_recv.at[2])
-        await_bytes(hid.at[0:3, :, 0, L:], ag_recv.at[3])
-        remote(hid.at[:, :, c], hid.at[:, :, c], ag_send.at[4], ag_recv.at[4], (d + 1 - 2 * c, t))
-        await_bytes(hid.at[:, :, 0], ag_recv.at[4])
-
-    def multiply():
-        prod[...] = jnp.zeros_like(prod)
-
-        @pl.loop(0, NDP)
+        for j in range(2, 4):
+            await_bytes(hid.at[0:3, :, 0, 0 : pieces[j][1]], ag_recv.at[4 + j])
+        await_bytes(hid.at[:, :, 0, 0 : 3 * quarter], ag_recv.at[8])
+        remote(hid.at[:, :, c], hid.at[:, :, c], ag_send.at[9], ag_recv.at[9], (d + 1 - 2 * c, t))
+
+    def multiply_half(core):
+        @pl.loop(0, 4)
         def _(i):
-            cols = pl.ds(pl.multiple_of(i * F, F), F)
-            rows = jnp.concatenate(
-                [shifted[p][:, :, cols].reshape(PARTS[p] * TILE, F) for p in range(NP)], axis=0
-            )
-            part = lax.dot_general(
-                rows, hid[i // 8, (i // 2) % 4, i % 2], (((1,), (1,)), ((), ())), preferred_element_type=F32
-            )
+            part = jnp.zeros((CHUNK * TILE, 2 * L), F32)
+            for j in range(4):
+                cols = pl.ds(pl.multiple_of((i * 8 + j * 2 + core) * F, F), F)
+                rows = jnp.concatenate(
+                    [shifted[p][:, :, cols].reshape(PARTS[p] * TILE, F) for p in range(NP)], axis=0
+                )
+                part += lax.dot_general(
+                    rows, hid[i, j, core], (((1,), (1,)), ((), ())), preferred_element_type=F32
+                )
             for s in range(2):
                 prod[s, 0:CHUNK] += part[:, s * L : (s + 1) * L].reshape(CHUNK, TILE, L)
+
+    def multiply():
+        multiply_half(c)
+        await_bytes(hid.at[:, :, 0], ag_recv.at[9])
+        multiply_half(1 - c)
 
     def product_tiles(i):
         low = (i // 2 + 16 * NDP * NT * CHUNK - first_tile(chunk)) % 16
@@ -544,6 +587,7 @@
             v = jnp.concatenate(values[2 * s : 2 * s + 2], axis=0) * scale[s : s + 1]
             mixed_ref[s * L : (s + 1) * L] = (v.T * gain).astype(BF16)
 
+    prod[...] = jnp.zeros_like(prod)
     zero = jnp.zeros((TILE, L), F32)
     bcbuf[ZERO_B] = jnp.zeros((TILE, F), BF16)
     gather[ZERO_R] = jnp.zeros((TILE, F), BF16)
@@ -552,27 +596,31 @@
     gather_first()
     loading[0].wait()
     shift_part(0)
+    gather_second()
     send_part(0)
-    gather_second()
+    gather_planes()
     shift_part(1)
     send_part(1)
     shift_part(2)
     shift_part(3)
+    shift_part(4)
     for cp in loading[1:]:
         cp.wait()
     find_windows(off_ref, own_ref, *[Table(table_ref, int(i)) for i in BASES], windows_ref)
-    forward_part(0)
     gather_third()
     multiply()
     send_products()
     send_part(2)
+    forward_part(0)
     forward_part(1)
+    send_part(3)
     forward_products()
-    send_part(3)
+    send_part(4)
     forward_part(2)
     send_heads()
+    forward_part(3)
     share_products()
-    forward_part(3)
+    forward_part(4)
     forward_dt()
     mix()
     share_common()
@@ -582,11 +630,11 @@
         cp.wait()
     for p in range(NP):
         await_bytes(shifted[p].at[:, :, 0 : (NDP - 1) * F], dp_send.at[p])
-    await_bytes(hid.at[0:3, 0, 0, 0:L], ag_send.at[0])
-    await_bytes(hid.at[0:3, 0, 0, L:], ag_send.at[1])
-    await_bytes(hid.at[0:3, :, 0, 0:L], ag_send.at[2])
-    await_bytes(hid.at[0:3, :, 0, L:], ag_send.at[3])
-    await_bytes(hid.at[:, :, 0], ag_send.at[4])
+    for j, (_, size, _, _) in enumerate(pieces):
+        await_bytes(hid.at[0:3, 0, 0, 0:size], ag_send.at[j])
+        await_bytes(hid.at[0:3, :, 0, 0:size], ag_send.at[4 + j])
+    await_bytes(hid.at[:, :, 0, 0 : 3 * quarter], ag_send.at[8])
+    await_bytes(hid.at[:, :, 0], ag_send.at[9])
     await_bytes(precv.at[0 : 2 * (NDP - 1)], p_send.at[0])
     await_bytes(brecv.at[1, :, 0:15], p_send.at[1])
     await_bytes(brecv.at[1], p_send.at[4])
@@ -641,20 +689,20 @@
             pltpu.VMEM((2, 3, 16, TILE, L), F32),
             pltpu.VMEM((8, L), F32),
             pltpu.VMEM((16, 8, L), F32),
-            dma((5,)),
-            dma((5,)),
+            dma((10,)),
+            dma((10,)),
             dma((5,)),
             dma((5,)),
             dma((NT - 1, 2)),
             dma((NT - 1, 2)),
-            dma((3,)),
+            dma((4,)),
             pltpu.VMEM((ZERO_B + 1, TILE, F), BF16),
             pltpu.VMEM((NT, 2 * WIDTH, TILE, F), BF16),
             pltpu.VMEM((ZERO_R + 1, TILE, F), BF16),
             pltpu.VMEM((NT, 16, TILE, F), BF16),
-            dma((NT - 1,)),
-            dma((NT - 1,)),
-            dma((1,)),
+            dma((NT - 1, 4)),
+            dma((NT - 1, 4)),
+            dma((4,)),
             pltpu.SMEM((5,), jnp.int32),
             pltpu.SMEM((G,), jnp.int32),
             pltpu.SMEM(TABLES.shape, jnp.int32),
@@ -679,23 +727,26 @@
     step = pl.program_id(0)
     g = owner_groups(own_ref, lax.axis_index("tensor"))
 
-    def tile(slot, block, tau):
-        at = (block * BT + tau) * 2
-        one, two = place_ref[at], place_ref[at + 1]
-        base = slot * SLOT
-        first = got_ref[one + base]
-        second = got_ref[jnp.maximum(two, 0) + base]
-        return first + jnp.where(two >= 0, second, jnp.zeros_like(second))
-
     @pl.when(step < 8)
     def _():
         k = step // 4
         gk = jnp.where(k == 0, g[0], g[1])
         for seg in range(2):
             block = off_ref[seg] // 2048 + gk
-            for j in range(8):
-                for q in range(4):
-                    out_ref[j * 8 + seg * 4 + q] = tile(2 * seg + k, block, (step % 4) * 32 + 4 * j + q)
+            slot = (2 * seg + k) * SLOT
+            first = block * BT + (step % 4) * 32
+            for j in range(0, 8, 2):
+                tiles = [got_ref[place_ref[first + 4 * j + q] + slot] for q in range(8)]
+                for q in range(8):
+                    out_ref[(j + q // 4) * 8 + seg * 4 + q % 4] = tiles[q]
+            for n in range(FIXES):
+                at = BLOCKS * BT + ((block * 4 + step % 4) * FIXES + n) * 3
+                q = place_ref[at]
+
+                @pl.when(q >= 0)
+                def _():
+                    both = got_ref[place_ref[at + 1] + slot] + got_ref[place_ref[at + 2] + slot]
+                    out_ref[(q // 4) * 8 + seg * 4 + q % 4] = both
 
     @pl.when(step == 8)
     def _():
@@ -711,7 +762,7 @@
 
 def place(offsets, group_owner, got, bc, dt):
     smem = pl.BlockSpec(memory_space=pltpu.SMEM)
-    table = jnp.asarray(PLACE.reshape(-1))
+    table = jnp.asarray(np.concatenate([PLACE[:, :, 0].reshape(-1), FIX.reshape(-1)]))
     got = got.reshape(NT * 4 * SLOT, TILE, F)
     rows = pl.pallas_call(
         place_kernel,

time: 130 us -> 126 us (0.969); the launches traced: 130 us -> 124 us
  Pallas kernels: 128 us -> 123 us
    pallas_call x1, Pallas kernels: 122 us -> 117 us  [exchange(): pl.pallas_call(exchange_kernel, out_shape=(pltpu.VMEM((NT, 4, SLOT, TILE,...]
where the time goes in v5:
time: 126 us; the launch traced here: 124 us
  Pallas kernels  123 us (98%)
    pallas_call x1, Pallas kernels, exchange(): pl.pallas_call(exchange_kernel, out_shape=(pltpu.VMEM((NT, 4, SLOT, TILE,...  117 us
    pallas_call x1, Pallas kernels, place(): pl.pallas_call(place_kernel, grid=(10,), out_shape=jax.ShapeDtypeStruct((...  5.68 us

profile of v5, /device:TPU:1, one launch (start us, length us, event | category | flops | bytes accessed | tf_op | source)
XLA Modules:
  0.0 124.0 jit_solution(14898233535550291949)
XLA Ops:
  0.6 0.0 copy-start
  0.6 0.0 copy-start.2
  0.7 0.0 copy-start.1
  0.7 117.0 %exchange.1 = (bf16[4,4,38,16,256]{4,3,2,1,0:T(8,128)(2,1)S(1)}, bf16[4,16,16,256]{3,2,1,0:T(8,128)(2,1)S(1)}, bf16[4,4,16,256]{3,2,1,0:T(8,128)(2,1)S(1)}, bf16[256,128]{1,0:T(8,128)(2,1)}) custom-call(s32[5]{0:T(128)} %off_ref.1, s32[8]{0:T(128)} %own_ref.1, s32[15912]{0:T(1024)} %constant.4.clone.table_hbm, f32[256]{0:T(256)} %rate_hbm.1, f32[256]{0:T(256)} %bias_hbm.1, ...), custom_call_target="tpu_custom_call" | custom-call | tf_op jit(solution)/shard_map/exchange/pallas_call | solution.py:658
  117.7 0.0 copy-done
  117.7 0.0 copy-done.2
  117.7 0.0 copy-done.1
  117.7 0.0 copy-start.3
  117.7 5.7 %place.1 = bf16[580,16,256]{2,1,0:T(8,128)(2,1)} custom-call(s32[5]{0:T(128)S(1)} %copy-done.1, s32[8]{0:T(128)S(1)} %copy-done.2, s32[2736]{0:T(1024)S(1)} %copy-done, bf16[608,16,256]{2,1,0:T(8,128)(2,1)S(1)} %bitcast.5, bf16[4,16,16,256]{3,2,1,0:T(8,128)(2,1)S(1)} %get-tuple-element.7.bc_ref, bf16[4,4,16,256]{3,2,1,0:T(8,128)(2,1)S(1)} %get-tuple-element.8.dt_ref), custom_call_target="tpu_custom_call" | custom-call | tf_op jit(solution)/shard_map/place/pallas_call | solution.py:767
  123.4 0.0 copy-done.3
  123.4 0.6 copy.13
Async XLA Ops:
  0.6 117.0 %copy-start = (s32[2736]{0:T(1024)S(1)}, s32[2736]{0:T(1024)}, u32[]{:S(2)}) copy-start(s32[2736]{0:T(1024)} %constant.5.clone.place_ref) | copy-start | bytes 32836
  0.6 117.0 %copy-start.2 = (s32[8]{0:T(128)S(1)}, s32[8]{0:T(128)}, u32[]{:S(2)}) copy-start(s32[8]{0:T(128)} %own_ref.1) | copy-start | bytes 100
  0.7 117.0 %copy-start.1 = (s32[5]{0:T(128)S(1)}, s32[5]{0:T(128)}, u32[]{:S(2)}) copy-start(s32[5]{0:T(128)} %off_ref.1) | copy-start | bytes 64
  117.7 5.7 %copy-start.3 = (bf16[256,128]{1,0:T(8,128)(2,1)S(1)}, bf16[256,128]{1,0:T(8,128)(2,1)}, u32[]{:S(2)}) copy-start(bf16[256,128]{1,0:T(8,128)(2,1)} %get-tuple-element.13) | copy-start | bytes 196612

commit v6 on v5

--- a/solution.py
+++ b/solution.py
@@ -723,60 +723,58 @@
 STEP = 64
 
 
-def place_kernel(off_ref, own_ref, place_ref, got_ref, bc_ref, dt_ref, out_ref):
-    step = pl.program_id(0)
+def place_kernel(off_ref, own_ref, place_ref, got_ref, bc_ref, dt_ref, rows_ref, out_ref, sem):
     g = owner_groups(own_ref, lax.axis_index("tensor"))
-
-    @pl.when(step < 8)
-    def _():
-        k = step // 4
-        gk = jnp.where(k == 0, g[0], g[1])
-        for seg in range(2):
-            block = off_ref[seg] // 2048 + gk
-            slot = (2 * seg + k) * SLOT
-            first = block * BT + (step % 4) * 32
-            for j in range(0, 8, 2):
-                tiles = [got_ref[place_ref[first + 4 * j + q] + slot] for q in range(8)]
-                for q in range(8):
-                    out_ref[(j + q // 4) * 8 + seg * 4 + q % 4] = tiles[q]
-            for n in range(FIXES):
-                at = BLOCKS * BT + ((block * 4 + step % 4) * FIXES + n) * 3
-                q = place_ref[at]
-
-                @pl.when(q >= 0)
-                def _():
-                    both = got_ref[place_ref[at + 1] + slot] + got_ref[place_ref[at + 2] + slot]
-                    out_ref[(q // 4) * 8 + seg * 4 + q % 4] = both
-
-    @pl.when(step == 8)
-    def _():
-        for n in range(4):
-            for q in range(16):
-                out_ref[n * 16 + q] = bc_ref[q % 4, n * 4 + q // 4]
-
-    @pl.when(step == 9)
-    def _():
-        for j in range(4):
-            out_ref[j] = dt_ref[3, j]
+    writes = []
+
+    def write(first, size):
+        tiles = pl.ds(first, size)
+        cp = pltpu.make_async_copy(out_ref.at[tiles], rows_ref.at[tiles], sem.at[len(writes)])
+        cp.start()
+        writes.append(cp)
+
+    for n in range(4):
+        for q in range(16):
+            out_ref[512 + n * 16 + q] = bc_ref[q % 4, n * 4 + q // 4]
+    for j in range(4):
+        out_ref[576 + j] = dt_ref[3, j]
+    write(512, 68)
+    for k in range(2):
+        for quarter in range(4):
+            base = (k * 4 + quarter) * STEP
+            for seg in range(2):
+                block = off_ref[seg] // 2048 + g[k]
+                slot = (2 * seg + k) * SLOT
+                first = block * BT + quarter * 32
+                for j in range(0, 8, 2):
+                    tiles = [got_ref[place_ref[first + 4 * j + q] + slot] for q in range(8)]
+                    for q in range(8):
+                        out_ref[base + (j + q // 4) * 8 + seg * 4 + q % 4] = tiles[q]
+                for n in range(FIXES):
+                    at = BLOCKS * BT + ((block * 4 + quarter) * FIXES + n) * 3
+                    q = place_ref[at]
+
+                    @pl.when(q >= 0)
+                    def _():
+                        both = got_ref[place_ref[at + 1] + slot] + got_ref[place_ref[at + 2] + slot]
+                        out_ref[base + (q // 4) * 8 + seg * 4 + q % 4] = both
+
+            write(base, STEP)
+    for cp in writes:
+        cp.wait()
 
 
 def place(offsets, group_owner, got, bc, dt):
     smem = pl.BlockSpec(memory_space=pltpu.SMEM)
+    vmem = pl.BlockSpec(memory_space=pltpu.VMEM)
     table = jnp.asarray(np.concatenate([PLACE[:, :, 0].reshape(-1), FIX.reshape(-1)]))
     got = got.reshape(NT * 4 * SLOT, TILE, F)
     rows = pl.pallas_call(
         place_kernel,
-        grid=(10,),
         out_shape=jax.ShapeDtypeStruct((580, TILE, F), BF16),
-        in_specs=[
-            smem,
-            smem,
-            smem,
-            pl.BlockSpec(memory_space=pltpu.VMEM),
-            pl.BlockSpec(memory_space=pltpu.VMEM),
-            pl.BlockSpec(memory_space=pltpu.VMEM),
-        ],
-        out_specs=pl.BlockSpec((STEP, TILE, F), lambda i: (i, 0, 0)),
+        in_specs=[smem, smem, smem, vmem, vmem, vmem],
+        out_specs=pl.BlockSpec(memory_space=pl.ANY),
+        scratch_shapes=[pltpu.VMEM((580, TILE, F), BF16), pltpu.SemaphoreType.DMA((9,))],
         compiler_params=pltpu.CompilerParams(vmem_limit_bytes=16 << 20),
         name="place",
     )(offsets, group_owner, table, got, bc, dt)

time: 126 us -> 123 us (0.976)
  Pallas kernels: 123 us -> 120 us
    pallas_call x1, Pallas kernels: 5.68 us -> 3.03 us  [place(): pl.pallas_call(place_kernel, out_shape=jax.ShapeDtypeStruct((580, TILE, F...]
where the time goes in v6:
time: 123 us; the launch traced here: 121 us
  Pallas kernels  120 us (98%)
    pallas_call x1, Pallas kernels, exchange(): pl.pallas_call(exchange_kernel, out_shape=(pltpu.VMEM((NT, 4, SLOT, TILE,...  117 us
    pallas_call x1, Pallas kernels, place(): pl.pallas_call(place_kernel, out_shape=jax.ShapeDtypeStruct((580, TILE, F...  3.03 us

profile of v6, /device:TPU:1, one launch (start us, length us, event | category | flops | bytes accessed | tf_op | source)
XLA Modules:
  0.0 121.4 jit_solution(15286249657420428623)
XLA Ops:
  0.6 0.0 copy-start
  0.6 0.0 copy-start.2
  0.7 0.0 copy-start.1
  0.7 117.0 %exchange.1 = (bf16[4,4,38,16,256]{4,3,2,1,0:T(8,128)(2,1)S(1)}, bf16[4,16,16,256]{3,2,1,0:T(8,128)(2,1)S(1)}, bf16[4,4,16,256]{3,2,1,0:T(8,128)(2,1)S(1)}, bf16[256,128]{1,0:T(8,128)(2,1)}) custom-call(s32[5]{0:T(128)} %off_ref.1, s32[8]{0:T(128)} %own_ref.1, s32[15912]{0:T(1024)} %constant.4.clone.table_hbm, f32[256]{0:T(256)} %rate_hbm.1, f32[256]{0:T(256)} %bias_hbm.1, ...), custom_call_target="tpu_custom_call" | custom-call | tf_op jit(solution)/shard_map/exchange/pallas_call | solution.py:658
  117.7 0.0 copy-done
  117.7 0.0 copy-done.2
  117.7 0.0 copy-done.1
  117.7 0.0 copy-start.3
  117.7 3.0 %place.1 = bf16[580,16,256]{2,1,0:T(8,128)(2,1)} custom-call(s32[5]{0:T(128)S(1)} %copy-done.1, s32[8]{0:T(128)S(1)} %copy-done.2, s32[2736]{0:T(1024)S(1)} %copy-done, bf16[608,16,256]{2,1,0:T(8,128)(2,1)S(1)} %bitcast.5, bf16[4,16,16,256]{3,2,1,0:T(8,128)(2,1)S(1)} %get-tuple-element.7.bc_ref, bf16[4,4,16,256]{3,2,1,0:T(8,128)(2,1)S(1)} %get-tuple-element.8.dt_ref), custom_call_target="tpu_custom_call" | custom-call | tf_op jit(solution)/shard_map/place/pallas_call | solution.py:772
  120.7 0.0 copy-done.3
  120.7 0.6 copy.13
Async XLA Ops:
  0.6 117.0 %copy-start = (s32[2736]{0:T(1024)S(1)}, s32[2736]{0:T(1024)}, u32[]{:S(2)}) copy-start(s32[2736]{0:T(1024)} %constant.5.clone.place_ref) | copy-start | bytes 32836
  0.6 117.0 %copy-start.2 = (s32[8]{0:T(128)S(1)}, s32[8]{0:T(128)}, u32[]{:S(2)}) copy-start(s32[8]{0:T(128)} %own_ref.1) | copy-start | bytes 100
  0.7 117.0 %copy-start.1 = (s32[5]{0:T(128)S(1)}, s32[5]{0:T(128)}, u32[]{:S(2)}) copy-start(s32[5]{0:T(128)} %off_ref.1) | copy-start | bytes 64
  117.7 3.0 %copy-start.3 = (bf16[256,128]{1,0:T(8,128)(2,1)S(1)}, bf16[256,128]{1,0:T(8,128)(2,1)}, u32[]{:S(2)}) copy-start(bf16[256,128]{1,0:T(8,128)(2,1)} %get-tuple-element.13) | copy-start | bytes 196612

commit v7 on v6

--- a/solution.py
+++ b/solution.py
@@ -453,7 +453,9 @@
                     rows, hid[i, j, core], (((1,), (1,)), ((), ())), preferred_element_type=F32
                 )
             for s in range(2):
-                prod[s, 0:CHUNK] += part[:, s * L : (s + 1) * L].reshape(CHUNK, TILE, L)
+                tiles = part[:, s * L : (s + 1) * L].reshape(CHUNK, TILE, L)
+                prod[s, 0] += tiles[:16]
+                prod[s, 1, 0 : CHUNK - 16] += tiles[16:]
 
     def multiply():
         multiply_half(c)
@@ -469,12 +471,10 @@
         def _(n):
             i = (d + n) % NDP
             low, s = product_tiles(i)
-            for h in range(2):
-                remote(prod.at[s, low + 16 * h], precv.at[2 * d + h], p_send.at[0], p_recv.at[0], (i, t))
+            remote(prod.at[s, :, low], precv.at[pl.ds(2 * d, 2)], p_send.at[0], p_recv.at[0], (i, t))
 
         low, s = product_tiles(d)
-        for h in range(2):
-            pltpu.make_async_copy(prod.at[s, low + 16 * h], precv.at[2 * d + h], p_recv.at[0]).start()
+        pltpu.make_async_copy(prod.at[s, :, low], precv.at[pl.ds(2 * d, 2)], p_recv.at[0]).start()
 
     def forward_products():
         await_bytes(precv.at[0 : 2 * NDP], p_recv.at[0])
@@ -678,7 +678,7 @@
             dma((NT - 1, NP + 2)),
             dma((NP + 2,)),
             pltpu.VMEM((4, 4, 2, 2 * L, F), BF16),
-            pltpu.VMEM((2, 32, TILE, L), F32),
+            pltpu.VMEM((2, 2, 16, TILE, L), F32),
             pltpu.VMEM((ZERO2 + 1, TILE, L), F32),
             pltpu.VMEM((NT, 4 * PICKS, TILE, L), F32),
             pltpu.VMEM((2 * PICKS + 1, TILE, L), F32),

time: 123 us -> 123 us (level)
  no operation moved by 1% of the time
where the time goes in v7:
time: 123 us; the launch traced here: 121 us
  Pallas kernels  120 us (98%)
    pallas_call x1, Pallas kernels, exchange(): pl.pallas_call(exchange_kernel, out_shape=(pltpu.VMEM((NT, 4, SLOT, TILE,...  117 us
    pallas_call x1, Pallas kernels, place(): pl.pallas_call(place_kernel, out_shape=jax.ShapeDtypeStruct((580, TILE, F...  3.03 us

profile of v7, /device:TPU:1, one launch (start us, length us, event | category | flops | bytes accessed | tf_op | source)
XLA Modules:
  0.0 121.4 jit_solution(5507485294330522487)
XLA Ops:
  0.6 0.0 copy-start
  0.6 0.0 copy-start.2
  0.7 0.0 copy-start.1
  0.7 117.0 %exchange.1 = (bf16[4,4,38,16,256]{4,3,2,1,0:T(8,128)(2,1)S(1)}, bf16[4,16,16,256]{3,2,1,0:T(8,128)(2,1)S(1)}, bf16[4,4,16,256]{3,2,1,0:T(8,128)(2,1)S(1)}, bf16[256,128]{1,0:T(8,128)(2,1)}) custom-call(s32[5]{0:T(128)} %off_ref.1, s32[8]{0:T(128)} %own_ref.1, s32[15912]{0:T(1024)} %constant.4.clone.table_hbm, f32[256]{0:T(256)} %rate_hbm.1, f32[256]{0:T(256)} %bias_hbm.1, ...), custom_call_target="tpu_custom_call" | custom-call | tf_op jit(solution)/shard_map/exchange/pallas_call | solution.py:658
  117.7 0.0 copy-done
  117.7 0.0 copy-done.2
  117.7 0.0 copy-done.1
  117.7 0.0 copy-start.3
  117.7 3.0 %place.1 = bf16[580,16,256]{2,1,0:T(8,128)(2,1)} custom-call(s32[5]{0:T(128)S(1)} %copy-done.1, s32[8]{0:T(128)S(1)} %copy-done.2, s32[2736]{0:T(1024)S(1)} %copy-done, bf16[608,16,256]{2,1,0:T(8,128)(2,1)S(1)} %bitcast.5, bf16[4,16,16,256]{3,2,1,0:T(8,128)(2,1)S(1)} %get-tuple-element.7.bc_ref, bf16[4,4,16,256]{3,2,1,0:T(8,128)(2,1)S(1)} %get-tuple-element.8.dt_ref), custom_call_target="tpu_custom_call" | custom-call | tf_op jit(solution)/shard_map/place/pallas_call | solution.py:772
  120.7 0.0 copy-done.3
  120.7 0.6 copy.13
Async XLA Ops:
  0.6 117.0 %copy-start = (s32[2736]{0:T(1024)S(1)}, s32[2736]{0:T(1024)}, u32[]{:S(2)}) copy-start(s32[2736]{0:T(1024)} %constant.5.clone.place_ref) | copy-start | bytes 32836
  0.6 117.0 %copy-start.2 = (s32[8]{0:T(128)S(1)}, s32[8]{0:T(128)}, u32[]{:S(2)}) copy-start(s32[8]{0:T(128)} %own_ref.1) | copy-start | bytes 100
  0.7 117.0 %copy-start.1 = (s32[5]{0:T(128)S(1)}, s32[5]{0:T(128)}, u32[]{:S(2)}) copy-start(s32[5]{0:T(128)} %off_ref.1) | copy-start | bytes 64
  117.7 3.0 %copy-start.3 = (bf16[256,128]{1,0:T(8,128)(2,1)S(1)}, bf16[256,128]{1,0:T(8,128)(2,1)}, u32[]{:S(2)}) copy-start(bf16[256,128]{1,0:T(8,128)(2,1)} %get-tuple-element.13) | copy-start | bytes 196612
